TPU v7x, 32 devices: a whole 2x2x4 slice. The times are simulated.
32 devices in a mesh: ti: 8 (over z, x), kz: 4 (over y, core).
Axes of the slice: x: 2, y: 2, z: 4, core: 2. Of those that a mesh axis runs over, the one named last changes fastest.
Arguments:
- point_maps: float32 [3, 4, 160, 256], P(None, None, 'kz'), may hold values from 0.3 to 3, as said below
- point_coils: float32 [2, 8, 4, 160, 256], P(None, None, None, 'kz'), may hold values from -2 to 2
- direction_maps: float32 [3, 4, 160, 256], P(None, None, 'kz', 'ti'), may hold values from -12 to 12
- direction_coils: float32 [2, 8, 4, 160, 256], P(None, None, None, 'kz', 'ti'), may hold values from -12 to 12
- residual_maps: float32 [3, 4, 160, 256], P(None, None, 'kz', 'ti'), may hold values from -12 to 12
- residual_coils: float32 [2, 8, 4, 160, 256], P(None, None, None, 'kz', 'ti'), may hold values from -12 to 12
- inversion_times: float32 [16], P('ti'), may hold values from 0.05 to 3
- sampling_mask: int32 [16, 160, 256], P('ti'), may hold values 0 or 1
Outputs:
- new_residual_maps: float32 [3, 4, 160, 256], P(None, None, 'kz', 'ti')
- new_residual_coils: float32 [2, 8, 4, 160, 256], P(None, None, None, 'kz', 'ti')
- new_direction_maps: float32 [3, 4, 160, 256], P(None, None, 'kz', 'ti')
- new_direction_coils: float32 [2, 8, 4, 160, 256], P(None, None, None, 'kz', 'ti')
Inputs may be any that keep to these rules, and one draw needn't show every extreme that they name: `sampling_mask`: 1 where the sample of that bin was acquired. `point_maps`: component 1 lies between 1.4 and 2 times component 0.
All inputs are finite; a program needn't handle non-finite values. No bound on the sum of `sampling_mask` on one device may be relied on, other than what follows from the above.
Results may differ from a plain program's by a relative error of at most 0.0003.
Values sent between devices are 32-bit elements; how exact they have to be, the bound alone decides.
A program may use at most 128 MiB of HBM per device.

v0:
```python
from functools import partial
import math

import jax
import jax.numpy as jnp
from jax import lax
from jax.sharding import PartitionSpec as P

regular_weight = 2.0


def dft_tables(length, orient):
    indices = jnp.arange(length, dtype=jnp.int32)
    phases = indices[:, None] * indices[None, :] % length
    angles = phases.astype(jnp.float32) * (2.0 * math.pi / length)
    factor = 1.0 / math.sqrt(length)
    return (jnp.cos(angles) * factor, orient * jnp.sin(angles) * factor)


def along_last(real_part, imag_part, tables):
    cos_part, sin_part = tables
    matmul = partial(jnp.dot, precision=lax.Precision.HIGHEST, preferred_element_type=jnp.float32)
    new_real = matmul(real_part, cos_part) - matmul(imag_part, sin_part)
    new_imag = matmul(real_part, sin_part) + matmul(imag_part, cos_part)
    return (new_real, new_imag)


def along_second(real_part, imag_part, tables):
    cos_part, sin_part = tables

    def contract(matrix, values):
        return jnp.einsum(
            "kz,...zy->...ky",
            matrix,
            values,
            precision=lax.Precision.HIGHEST,
            preferred_element_type=jnp.float32,
        )

    new_real = contract(cos_part, real_part) - contract(sin_part, imag_part)
    new_imag = contract(cos_part, imag_part) + contract(sin_part, real_part)
    return (new_real, new_imag)


def inner_sum(left_side, right_side):
    return jnp.sum(left_side[0] * right_side[0]) + jnp.sum(left_side[1] * right_side[1])


def model_terms(maps, bin_times):
    decays = jnp.exp(-bin_times * maps[2][None])
    signal = maps[0][None] - maps[1][None] * decays
    return (decays, signal)


def gradients(returned, maps, coils, decays, signal, bin_times):
    back_re = returned[0]
    back_im = returned[1]
    projected = jnp.sum(coils[0][None] * back_re + coils[1][None] * back_im, axis=1)
    grad_maps = jnp.stack(
        [
            jnp.sum(projected, axis=0),
            -jnp.sum(decays * projected, axis=0),
            maps[1] * jnp.sum(bin_times * decays * projected, axis=0),
        ]
    )
    grad_coils = jnp.stack(
        [jnp.sum(signal[:, None] * back_re, axis=0), jnp.sum(signal[:, None] * back_im, axis=0)]
    )
    return (grad_maps, grad_coils)


def shards(
    point_maps,
    point_coils,
    direction_maps,
    direction_coils,
    residual_maps,
    residual_coils,
    inversion_times,
    sampling_mask,
):
    full_maps, full_coils = (
        lax.all_gather(direction_maps, "ti", axis=3, tiled=True),
        lax.all_gather(direction_coils, "ti", axis=4, tiled=True),
    )
    amplitude = point_maps[1]
    bin_times = inversion_times[:, None, None, None]
    decays, signal = model_terms(point_maps, bin_times)
    signal_step = (
        full_maps[0][None]
        - full_maps[1][None] * decays
        + amplitude[None] * bin_times * decays * full_maps[2][None]
    )
    image_re = point_coils[0][None] * signal_step[:, None] + full_coils[0][None] * signal[:, None]
    image_im = point_coils[1][None] * signal_step[:, None] + full_coils[1][None] * signal[:, None]
    images = jnp.stack([image_re, image_im])
    partitions = sampling_mask.shape[1]
    encodes = sampling_mask.shape[2]
    weights = sampling_mask.astype(jnp.float32)[:, None, None]
    forward_y = dft_tables(encodes, -1.0)
    backward_y = dft_tables(encodes, 1.0)
    forward_z = dft_tables(partitions, -1.0)
    backward_z = dft_tables(partitions, 1.0)
    received = lax.all_to_all(images, "kz", split_axis=3, concat_axis=4, tiled=True)
    real_part, imag_part = along_last(received[0], received[1], forward_y)
    real_part, imag_part = along_second(real_part, imag_part, forward_z)
    real_part = real_part * weights
    imag_part = imag_part * weights
    real_part, imag_part = along_last(real_part, imag_part, backward_y)
    real_part, imag_part = along_second(real_part, imag_part, backward_z)
    returned = lax.all_to_all(
        jnp.stack([real_part, imag_part]), "kz", split_axis=4, concat_axis=3, tiled=True
    )
    grad_maps, grad_coils = gradients(returned, point_maps, point_coils, decays, signal, bin_times)
    share_width = direction_maps.shape[3]
    total_maps, total_coils = lax.psum((grad_maps, grad_coils), "ti")
    offset = lax.axis_index("ti") * share_width
    share_maps = lax.dynamic_slice_in_dim(total_maps, offset, share_width, 3)
    share_coils = lax.dynamic_slice_in_dim(total_coils, offset, share_width, 4)
    applied_maps = share_maps + regular_weight * direction_maps
    applied_coils = share_coils + regular_weight * direction_coils
    directions = (direction_maps, direction_coils)
    residuals = (residual_maps, residual_coils)
    applied = (applied_maps, applied_coils)
    old_norm = lax.psum(inner_sum(residuals, residuals), ("ti", "kz"))
    curvature = lax.psum(inner_sum(directions, applied), ("ti", "kz"))
    step_size = old_norm / curvature
    new_residual_maps = residual_maps - step_size * applied_maps
    new_residual_coils = residual_coils - step_size * applied_coils
    updated = (new_residual_maps, new_residual_coils)
    new_norm = lax.psum(inner_sum(updated, updated), ("ti", "kz"))
    conjugacy = new_norm / old_norm
    new_direction_maps = new_residual_maps + conjugacy * direction_maps
    new_direction_coils = new_residual_coils + conjugacy * direction_coils
    return (new_residual_maps, new_residual_coils, new_direction_maps, new_direction_coils)


def solution(mesh):
    in_specs = (
        P(None, None, "kz", None),
        P(None, None, None, "kz", None),
        P(None, None, "kz", "ti"),
        P(None, None, None, "kz", "ti"),
        P(None, None, "kz", "ti"),
        P(None, None, None, "kz", "ti"),
        P("ti"),
        P("ti", None, None),
    )
    out_specs = (
        P(None, None, "kz", "ti"),
        P(None, None, None, "kz", "ti"),
        P(None, None, "kz", "ti"),
        P(None, None, None, "kz", "ti"),
    )
    return jax.shard_map(shards, mesh=mesh, in_specs=in_specs, out_specs=out_specs, check_vma=False)
```

profile of v0, /device:TPU:0, one launch (start us, length us, event | category | flops | bytes accessed | tf_op | source)
XLA Modules:
  0.0 610.1 jit_solution(4434482918615585904)
XLA Ops:
  8.6 47.7 %all_gather.6 = f32[3,4,40,256]{2,3,1,0:T(8,128)S(1)} all-gather(f32[3,4,40,32]{2,3,1,0:T(8,128)} %param.10), channel_id=1, replica_groups=mesh['ti'=8,'kz'=4] {'ti'}, dimensions={3}, use_global_device_ids=true | all-gather | bytes 552960 | tf_op jit(solution)/shard_map/all_gather | solution.py:83
  58.3 3.8 fusion.172
  62.1 89.2 %all-gather.2.cloned.1.call-done = f32[2,8,4,40,256]{3,4,2,1,0:T(8,128)} async-done(((f32[2,8,4,40,32]{3,4,2,1,0:T(8,128)}), f32[2,8,4,40,256]{3,4,2,1,0:T(8,128)}) %all-gather.2.cloned.1.call-update) | async-done | bytes 2621456 | tf_op jit(solution)/shard_map/all_gather | solution.py:84
  151.3 7.7 %slice_bitcast_fusion.1 = (f32[8,4,40,256]{2,3,1,0:T(8,128)}, f32[8,4,40,256]{2,3,1,0:T(8,128)}) fusion(f32[2,8,4,40,256]{3,4,2,1,0:T(8,128)} %all-gather.2.cloned.1.call-done), kind=kLoop, calls=%fused_computation.3 | loop fusion | bytes 5242880 | tf_op jit(solution)/shard_map/mul | solution.py:94
  159.0 3.7 copy.65
  162.7 3.7 copy.67
  166.4 3.3 multiply_add_fusion.2
  169.7 2.7 pad_maximum_fusion
  172.4 5.3 all-to-all-start
  177.8 59.3 %all-to-all-done = f32[2,2,8,4,40,256]{5,4,2,1,0,3:T(8,128)} async-done(((f32[2,2,8,4,40,256]{5,4,2,1,0,3:T(8,128)}), f32[2,2,8,4,40,256]{5,4,2,1,0,3:T(8,128)}, u32[]{:S(2)}, u32[]{:S(2)}) %all-to-all-start) | async-done | bytes 5242912 | tf_op jit(solution)/shard_map/all_to_all | solution.py:104
  237.0 2.9 fusion.171
  240.2 3.3 fusion.14
  243.5 3.2 fusion.12
  247.0 3.4 convolution_add_fusion.1
  250.4 3.6 convolution_subtract_fusion.1
  254.1 3.2 fusion.36
  257.3 3.2 fusion.34
  260.5 3.5 fusion.1
  264.0 3.7 fusion.5
  267.7 3.3 fusion.9
  271.0 3.5 fusion
  274.5 3.5 convolution_add_fusion
  278.0 3.4 convolution_subtract_fusion
  281.5 3.2 fusion.32
  284.7 3.2 fusion.30
  287.9 3.5 subtract_bitcast_fusion
  291.4 3.3 add_bitcast_fusion
  295.2 5.4 copy.70
  300.6 5.0 all-to-all-start.1
  306.0 1.9 copy.60
  307.9 1.8 copy.71
  310.1 55.1 %all-to-all-done.1 = f32[2,2,8,1,160,256]{5,2,1,3,0,4:T(8,128)} async-done(((f32[2,2,8,1,160,256]{5,2,1,3,0,4:T(8,128)}), f32[2,2,8,1,160,256]{5,2,1,3,0,4:T(8,128)}, u32[]{:S(2)}, u32[]{:S(2)}) %all-to-all-start.1) | async-done | bytes 5242912 | tf_op jit(solution)/shard_map/all_to_all | solution.py:111
  365.1 6.0 multiply_reduce_fusion.1
  371.5 1.1 multiply_reduce_fusion.6
  372.6 0.9 slice_multiply_fusion
  374.0 1.8 pad_maximum_fusion.2
  378.1 1.8 copy.78
  379.8 1.6 multiply_reduce_fusion.9
  381.4 0.9 multiply_reduce_fusion.4
  383.6 119.4 %all-reduce.4.cloned.1.call-done = (f32[3,4,40,256]{3,2,1,0:T(8,128)}, f32[2,8,4,40,256]{4,3,2,1,0:T(8,128)}) async-done(((f32[3,4,40,256]{3,2,1,0:T(8,128)}, f32[2,8,4,40,256]{4,3,2,1,0:T(8,128)}), (f32[3,4,40,256]{3,2,1,0:T(8,128)}, f32[2,8,4,40,256]{4,3,2,1,0:T(8,128)})) %all-reduce.4.cloned.1.call-update) | async-done | bytes 3112976 | tf_op jit(solution)/shard_map/psum | solution.py:116
  503.0 2.4 multiply_reduce_fusion.3
  507.5 1.5 copy.79
  509.0 39.0 %all-reduce = (f32[]{:T(128)}, f32[]{:T(128)}) all-reduce(f32[]{:T(128)S(6)} %add.137, f32[]{:T(128)S(6)} %add.155), channel_id=1, replica_groups=mesh['ti'=8,'kz'=4] {'ti','kz'}, use_global_device_ids=true, to_apply=%region_2.3 | all-reduce | flops 2 | bytes 16 | tf_op jit(solution)/shard_map/psum | solution.py:125
  549.3 2.8 multiply_reduce_fusion.2
  554.2 40.4 %psum.39 = f32[]{:T(128)} all-reduce(f32[]{:T(128)S(6)} %add.156), channel_id=1, replica_groups=mesh['ti'=8,'kz'=4] {'ti','kz'}, use_global_device_ids=true, to_apply=%region_16.17 | all-reduce | flops 1 | bytes 8 | tf_op jit(solution)/shard_map/psum | solution.py:131
  595.9 1.4 copy.83
  597.2 1.2 multiply_add_fusion.3
  599.3 2.7 copy.85
  (55 shorter events, 11.4 us)
Async XLA Ops:
  7.2 144.1 %all-gather.2.cloned.1.call-start = ((), (), s32[]{:S(2)}) async-start(), calls=%async_computation.2 | async-start | bytes 9437184 | tf_op jit(solution)/shard_map/all_gather | solution.py:84
  56.2 1.0 copy-start.6
  56.2 1.8 copy-start.13
  172.4 5.4 copy-start.12
  172.4 64.6 %all-to-all-start = ((f32[2,2,8,4,40,256]{5,4,2,1,0,3:T(8,128)}), f32[2,2,8,4,40,256]{5,4,2,1,0,3:T(8,128)}, u32[]{:S(2)}, u32[]{:S(2)}) async-start(f32[2,2,8,4,40,256]{5,4,2,1,0,3:T(8,128)} %pad_maximum_fusion), calls=%async_computation | async-start | bytes 10485760 | tf_op jit(solution)/shard_map/all_to_all | solution.py:104
  300.6 64.5 %all-to-all-start.1 = ((f32[2,2,8,1,160,256]{5,2,1,3,0,4:T(8,128)}), f32[2,2,8,1,160,256]{5,2,1,3,0,4:T(8,128)}, u32[]{:S(2)}, u32[]{:S(2)}) async-start(f32[2,2,8,1,160,256]{5,2,1,3,0,4:T(8,128)} %copy.70), calls=%async_computation.1 | async-start | bytes 10485760 | tf_op jit(solution)/shard_map/all_to_all | solution.py:111
  305.7 197.4 %all-reduce.4.cloned.1.call-start = ((), (), s32[]{:S(2)}) async-start(), calls=%async_computation.3 | async-start | bytes 6225920 | tf_op jit(solution)/shard_map/psum | solution.py:116
  306.0 3.7 copy-start.8
  306.0 3.7 copy-start.9
  307.9 57.3 %copy-start = (f32[8,160,256]{2,0,1:T(8,128)S(1)}, f32[8,160,256]{2,0,1:T(8,128)}, u32[]{:S(2)}) copy-start(f32[8,160,256]{2,0,1:T(8,128)} %copy.60) | copy-start | bytes 3932164
  375.8 1.0 copy-start.7
  375.8 1.8 copy-start.1
  376.6 4.9 copy-start.2
  378.0 127.4 %copy-start.3 = (f32[3,4,40,32]{3,2,1,0:T(8,128)S(1)}, f32[3,4,40,32]{3,2,1,0:T(8,128)}, u32[]{:S(2)}) copy-start(f32[3,4,40,32]{3,2,1,0:T(8,128)} %copy.73) | copy-start | bytes 184324
  503.0 2.4 copy-start.10
  549.3 2.8 copy-start.4
  549.3 2.8 copy-start.5
  549.3 2.8 copy-start.11
Sparse Core Ops, SparseCore 0:
  10.2 141.0 all-gather.1
  376.7 126.2 all-reduce.3
where the time goes:
time: 614 us; the launch traced here: 610 us
  waiting for transfers between devices  324 us (53%)
  blocking collectives  127 us (21%)
  matrix products  54.1 us (9%)
  local copies, waits for them, and re-layouts  44.6 us (7%)
  other arithmetic  28.7 us (5%)
  between operations  21.4 us (3%)
  starting transfers between devices  10.7 us (2%)
    psum x1, waiting for transfers between devices, shards(): total_maps, total_coils = lax.psum((grad_maps, grad_coils), 'ti')  119 us
    all_gather x1, waiting for transfers between devices, shards(): lax.all_gather(direction_coils, 'ti', axis=4, tiled=True)  89.2 us
    all_to_all x1, waiting for transfers between devices, shards(): lax.all_to_all(images, 'kz', split_axis=3, concat_axis=4, tiled=True)  59.3 us
    all_to_all x1, waiting for transfers between devices, shards(): lax.all_to_all(jnp.stack([real_part, imag_part]), 'kz', split_axis=4, con...  55.1 us
    all_gather x1, blocking collectives, shards(): lax.all_gather(direction_maps, 'ti', axis=3, tiled=True)  47.7 us
    psum x1, blocking collectives, shards(): new_norm = lax.psum(inner_sum(updated, updated), ('ti', 'kz'))  40.4 us
    psum x1, blocking collectives, shards(): old_norm = lax.psum(inner_sum(residuals, residuals), ('ti', 'kz'))  39 us
    dot_general x8, matrix products, contract(): jnp.einsum('kz,...zy->...ky', matrix, values, precision=lax.Precision.HIG...  26.6 us
  transfers between devices with their start and end apart: 4, of which 4 were waited for; matrix products, arithmetic and copies ran while one was open for 3% of the time, Pallas kernels for 0%

commit v1 on v0

v1 whole, which is shorter than its diff:
```python
import functools
import math

import jax
import jax.numpy as jnp
import ml_dtypes
import numpy as np
from jax import lax
from jax.experimental import pallas as pl
from jax.experimental.pallas import tpu as pltpu
from jax.sharding import PartitionSpec as P

MESH = pl.DeviceIdType.MESH
regular_weight = 2.0
COIL_GROUPS = 4
LANES = 128
VMEM_LIMIT = 48 * 1024 * 1024


def split_table(table):
    high = table.astype(ml_dtypes.bfloat16)
    low = (table - high.astype(np.float64)).astype(ml_dtypes.bfloat16)
    return np.stack([high, low])


def dft_parts(length):
    indices = np.arange(length)
    angles = (indices[:, None] * indices[None, :] % length) * (2.0 * math.pi / length)
    factor = 1.0 / math.sqrt(length)
    return np.cos(angles) * factor, np.sin(angles) * factor


def tables_y(length):
    c, s = dft_parts(length)
    forward = np.block([[c, -s], [s, c]])
    backward = np.block([[c, s], [-s, c]])
    return split_table(forward), split_table(backward)


def tables_z(length):
    c, s = dft_parts(length)
    forward = np.block([[c, s], [-s, c]])
    backward = np.block([[c, -s], [s, c]])
    return split_table(forward), split_table(backward)


def halves(values):
    high = values.astype(jnp.bfloat16)
    low = (values - high.astype(jnp.float32)).astype(jnp.bfloat16)
    return high, low


dot = functools.partial(jnp.dot, preferred_element_type=jnp.float32)


def from_right(values, table):
    high, low = halves(values)
    return dot(high, table[0]) + (dot(low, table[0]) + dot(high, table[1]))


def from_left(table, values):
    high, low = halves(values)
    return dot(table[0], high) + (dot(table[0], low) + dot(table[1], high))


def packed_coils(coils, x, group, per_group):
    parts = [coils[ri, group * per_group + c, x] for c in range(per_group) for ri in range(2)]
    return wide(jnp.concatenate(parts, axis=-1))


def packed_maps(maps, x):
    parts = [maps[m, x] for m in range(3)]
    return wide(jnp.concatenate(parts + [jnp.zeros_like(parts[0])], axis=-1))


def wide(values):
    missing = LANES - values.shape[-1]
    if missing:
        values = jnp.concatenate([values, jnp.zeros((values.shape[0], missing), values.dtype)], axis=-1)
    return values


def enter(n_ti, n_kz, me):
    total = n_ti * n_kz
    barrier = pltpu.get_barrier_semaphore()

    def greet(offset, carry):
        other = lax.rem(me + offset, total)
        pl.semaphore_signal(
            barrier, inc=1, device_id=(other // n_kz, lax.rem(other, n_kz)), device_id_type=MESH
        )
        return carry

    lax.fori_loop(1, total, greet, 0)
    return barrier


def gather_kernel(
    n_ti, n_kz, per_group,
    dir_maps, dir_coils, maps, coils, times, mask,
    got_dir, got_maps, got_coils, got_times, got_mask,
    send, dir_out, dir_in, map_out, map_in, coil_out, coil_in, time_out, time_in, mask_out, mask_in, own,
):
    total = n_ti * n_kz
    ti = lax.axis_index("ti")
    kz = lax.axis_index("kz")
    me = ti * n_kz + kz
    group = lax.rem(ti, COIL_GROUPS)
    first = (ti // COIL_GROUPS) * COIL_GROUPS
    barrier = enter(n_ti, n_kz, me)

    my_coils = pl.ds(group * per_group, per_group)
    locals_ = [
        pltpu.make_async_copy(maps.at[:, kz], got_maps.at[kz], own.at[0]),
        pltpu.make_async_copy(coils.at[:, my_coils, kz], got_coils.at[kz], own.at[1]),
        pltpu.make_async_copy(times, got_times.at[group], own.at[2]),
        pltpu.make_async_copy(mask, got_mask.at[group], own.at[3]),
    ]
    for copy in locals_:
        copy.start()

    for x in range(n_kz):
        packed = packed_maps(dir_maps, x)
        for g in range(COIL_GROUPS):
            send[x, g, 0] = packed_coils(dir_coils, x, g, per_group)
            send[x, g, 1] = packed
    own_dir = pltpu.make_async_copy(send.at[kz, group], got_dir.at[me], own.at[4])
    own_dir.start()

    pl.semaphore_wait(barrier, total - 1)

    def mask_copies(other, slot, sem):
        where = (first + other, kz)
        return [
            pltpu.make_async_remote_copy(
                mask, got_mask.at[slot], mask_out.at[other], mask_in.at[sem], device_id=where, device_id_type=MESH
            ),
            pltpu.make_async_remote_copy(
                times, got_times.at[slot], time_out.at[other], time_in.at[sem], device_id=where, device_id_type=MESH
            ),
        ]

    def point_copies(other, slot, sem):
        where = (ti, other)
        return [
            pltpu.make_async_remote_copy(
                maps.at[:, other], got_maps.at[slot], map_out.at[other], map_in.at[sem],
                device_id=where, device_id_type=MESH,
            ),
            pltpu.make_async_remote_copy(
                coils.at[:, my_coils, other], got_coils.at[slot], coil_out.at[other], coil_in.at[sem],
                device_id=where, device_id_type=MESH,
            ),
        ]

    def dir_copy(other, slot, sem):
        other_ti = other // n_kz
        other_kz = lax.rem(other, n_kz)
        return pltpu.make_async_remote_copy(
            send.at[other_kz, lax.rem(other_ti, COIL_GROUPS)], got_dir.at[slot],
            dir_out.at[other], dir_in.at[sem],
            device_id=(other_ti, other_kz), device_id_type=MESH,
        )

    def send_dir(offset, carry):
        dir_copy(lax.rem(me + offset, total), me, me).start()
        return carry

    lax.fori_loop(1, total, send_dir, 0)
    for offset in range(1, n_kz):
        for copy in point_copies(lax.rem(kz + offset, n_kz), kz, kz):
            copy.start()
    for offset in range(1, COIL_GROUPS):
        for copy in mask_copies(lax.rem(group + offset, COIL_GROUPS), group, group):
            copy.start()

    for copy in locals_:
        copy.wait()
    own_dir.wait()

    def wait_dir(offset, carry):
        other = lax.rem(me + offset, total)
        copy = dir_copy(other, other, other)
        copy.wait_send()
        copy.wait_recv()
        return carry

    lax.fori_loop(1, total, wait_dir, 0)
    for offset in range(1, n_kz):
        other = lax.rem(kz + offset, n_kz)
        for copy in point_copies(other, other, other):
            copy.wait_send()
            copy.wait_recv()
    for offset in range(1, COIL_GROUPS):
        other = lax.rem(group + offset, COIL_GROUPS)
        for copy in mask_copies(other, other, other):
            copy.wait_send()
            copy.wait_recv()


def lane_block(width):
    return lambda rows: lax.broadcasted_iota(jnp.int32, (rows, LANES), 1) // width


def transform_kernel(
    n_ti, n_kz, per_group, bins,
    got_dir, got_maps, got_coils, times, mask, y_forward, y_backward, z_forward, z_backward,
    out, step_maps, step_coils, maps, coils, grad_maps, grad_coils,
):
    t = pl.program_id(0)
    rows = got_dir.shape[2]
    nz = maps.shape[1]
    width = maps.shape[2] // n_ti
    per_tile = LANES // width
    tiles = maps.shape[2] // LANES
    block_of = lax.broadcasted_iota(jnp.int32, (rows, LANES), 1) // width

    @pl.when(t == 0)
    def _():
        grad_maps[...] = jnp.zeros_like(grad_maps)
        grad_coils[...] = jnp.zeros_like(grad_coils)
        for k in range(n_kz):
            span = slice(k * rows, (k + 1) * rows)
            for m in range(3):
                maps[m, span, :] = got_maps[k, m]
            for c in range(per_group):
                for ri in range(2):
                    coils[2 * c + ri, span, :] = got_coils[k, ri, c]
            for h in range(tiles):
                lanes = slice(h * LANES, (h + 1) * LANES)
                for pack, target, planes in ((0, step_coils, 4), (1, step_maps, 3)):
                    blocks = [got_dir[(h * per_tile + j) * n_kz + k, pack] for j in range(per_tile)]
                    for p in range(planes):
                        value = blocks[p % per_tile]
                        value = jnp.zeros((rows, LANES), jnp.float32)
                        for j in range(per_tile):
                            shift = ((j - p) * width) % LANES
                            moved = pltpu.roll(blocks[j], shift, 1) if shift else blocks[j]
                            value = jnp.where(block_of == j, moved, value)
                        target[p, span, lanes] = value

    tau = times[0, 0, 0:1, 0:1]
    amplitude = maps[1]
    decays = jnp.exp(-tau * maps[2])
    signal = maps[0] - amplitude * decays
    slope = amplitude * tau * decays
    signal_step = step_maps[0] - step_maps[1] * decays + slope * step_maps[2]
    kept = mask[0, 0].astype(jnp.float32)

    along_y = []
    for c in range(per_group):
        real = coils[2 * c] * signal_step + step_coils[2 * c] * signal
        imag = coils[2 * c + 1] * signal_step + step_coils[2 * c + 1] * signal
        along_y.append(jnp.concatenate([real, imag], axis=1))
    ny = real.shape[1]
    both = from_right(jnp.concatenate(along_y, axis=0), y_forward)
    along_z = jnp.concatenate(
        [
            jnp.concatenate([both[c * nz : (c + 1) * nz, :ny], both[c * nz : (c + 1) * nz, ny:]], axis=0)
            for c in range(per_group)
        ],
        axis=1,
    )
    kspace = from_left(z_forward, along_z)
    kept_all = jnp.concatenate([jnp.concatenate([kept] * per_group, axis=1)] * 2, axis=0)
    back = from_left(z_backward, kspace * kept_all)
    both = jnp.concatenate(
        [
            jnp.concatenate([back[:nz, c * ny : (c + 1) * ny], back[nz:, c * ny : (c + 1) * ny]], axis=1)
            for c in range(per_group)
        ],
        axis=0,
    )
    back = from_right(both, y_backward)
    projected = jnp.zeros_like(signal)
    for c in range(per_group):
        real = back[c * nz : (c + 1) * nz, :ny]
        imag = back[c * nz : (c + 1) * nz, ny:]
        projected += coils[2 * c] * real + coils[2 * c + 1] * imag
        grad_coils[2 * c] += signal * real
        grad_coils[2 * c + 1] += signal * imag
    grad_maps[0] += projected
    grad_maps[1] -= decays * projected
    grad_maps[2] += slope * projected

    @pl.when(t == bins - 1)
    def _():
        for k in range(n_kz):
            span = slice(k * rows, (k + 1) * rows)
            for h in range(tiles):
                lanes = slice(h * LANES, (h + 1) * LANES)
                for pack, source, planes in ((0, grad_coils, 4), (1, grad_maps, 3)):
                    blocks = [source[p, span, lanes] for p in range(planes)]
                    for j in range(per_tile):
                        value = jnp.zeros((rows, LANES), jnp.float32)
                        for p in range(planes):
                            shift = ((p - j) * width) % LANES
                            moved = pltpu.roll(blocks[p], shift, 1) if shift else blocks[p]
                            value = jnp.where(block_of == p, moved, value)
                        out[(h * per_tile + j) * n_kz + k, pack] = value


def update_kernel(
    n_ti, n_kz, per_group,
    grads, dir_maps, dir_coils, res_maps, res_coils,
    new_res_maps, new_res_coils, new_dir_maps, new_dir_coils,
    got, direction, residual, applied, sums, got_sums,
    grad_out, grad_in, sum_out, sum_in, own,
):
    total = n_ti * n_kz
    ti = lax.axis_index("ti")
    kz = lax.axis_index("kz")
    me = ti * n_kz + kz
    barrier = enter(n_ti, n_kz, me)
    own_grad = pltpu.make_async_copy(grads.at[me], got.at[me], own.at[0])
    own_grad.start()
    pl.semaphore_wait(barrier, total - 1)

    def grad_copy(other, slot):
        return pltpu.make_async_remote_copy(
            grads.at[other], got.at[slot], grad_out.at[other], grad_in.at[slot],
            device_id=(other // n_kz, lax.rem(other, n_kz)), device_id_type=MESH,
        )

    def sum_copy(other, slot):
        return pltpu.make_async_remote_copy(
            sums, got_sums.at[slot], sum_out.at[other], sum_in.at[slot],
            device_id=(other // n_kz, lax.rem(other, n_kz)), device_id_type=MESH,
        )

    def send_grad(offset, carry):
        grad_copy(lax.rem(me + offset, total), me).start()
        return carry

    lax.fori_loop(1, total, send_grad, 0)

    for x in range(n_kz):
        for g in range(COIL_GROUPS):
            direction[x, g] = packed_coils(dir_coils, x, g, per_group)
            residual[x, g] = packed_coils(res_coils, x, g, per_group)
        direction[x, COIL_GROUPS] = packed_maps(dir_maps, x)
        residual[x, COIL_GROUPS] = packed_maps(res_maps, x)

    own_grad.wait()

    def wait_grad(offset, carry):
        other = lax.rem(me + offset, total)
        copy = grad_copy(other, other)
        copy.wait_send()
        copy.wait_recv()
        return carry

    lax.fori_loop(1, total, wait_grad, 0)

    zeros = jnp.zeros(got.shape[2:], jnp.float32)
    old, bend, cross, square = zeros, zeros, zeros, zeros
    for x in range(n_kz):
        for g in range(COIL_GROUPS + 1):
            if g < COIL_GROUPS:
                terms = [got[t * n_kz + x, 0] for t in range(g, n_ti, COIL_GROUPS)]
            else:
                terms = [got[t * n_kz + x, 1] for t in range(n_ti)]
            d = direction[x, g]
            r = residual[x, g]
            a = functools.reduce(lambda u, v: u + v, terms) + regular_weight * d
            applied[x, g] = a
            old += r * r
            bend += d * a
            cross += r * a
            square += a * a
    row = lax.broadcasted_iota(jnp.int32, sums.shape, 0)
    tile = jnp.zeros(sums.shape, jnp.float32)
    for i, part in enumerate((old, bend, cross, square)):
        tile = jnp.where(row == i, jnp.sum(part, keepdims=True), tile)
    sums[...] = tile

    def send_sum(offset, carry):
        sum_copy(lax.rem(me + offset, total), me).start()
        return carry

    lax.fori_loop(1, total, send_sum, 0)
    got_sums[me] = tile

    def wait_sum(offset, carry):
        other = lax.rem(me + offset, total)
        copy = sum_copy(other, other)
        copy.wait_send()
        copy.wait_recv()
        return carry

    lax.fori_loop(1, total, wait_sum, 0)
    whole = jnp.sum(got_sums[...], axis=0)
    old, bend, cross, square = (whole[i : i + 1, :] for i in range(4))
    step = old / bend
    ratio = (old - 2.0 * step * cross + step * step * square) / old
    width = dir_maps.shape[-1]
    for x in range(n_kz):
        for g in range(COIL_GROUPS + 1):
            r = residual[x, g] - step * applied[x, g]
            d = r + ratio * direction[x, g]
            for p in range(4 if g < COIL_GROUPS else 3):
                lanes = slice(p * width, (p + 1) * width)
                if g < COIL_GROUPS:
                    new_res_coils[p % 2, g * per_group + p // 2, x] = r[:, lanes]
                    new_dir_coils[p % 2, g * per_group + p // 2, x] = d[:, lanes]
                else:
                    new_res_maps[p, x] = r[:, lanes]
                    new_dir_maps[p, x] = d[:, lanes]


def shards(
    n_ti, n_kz,
    point_maps, point_coils, direction_maps, direction_coils,
    residual_maps, residual_coils, inversion_times, sampling_mask,
):
    total = n_ti * n_kz
    coils = point_coils.shape[1]
    per_group = coils // COIL_GROUPS
    rows, ny = point_maps.shape[2:]
    local_bins, nz, _ = sampling_mask.shape
    bins = COIL_GROUPS * local_bins
    f32 = jnp.float32
    any_ = pl.BlockSpec(memory_space=pl.ANY)
    vmem = pl.BlockSpec(memory_space=pltpu.VMEM)
    dma = pltpu.SemaphoreType.DMA
    times = jnp.broadcast_to(inversion_times[:, None, None], (local_bins, 8, LANES))

    got_dir, got_maps, got_coils, got_times, got_mask = pl.pallas_call(
        functools.partial(gather_kernel, n_ti, n_kz, per_group),
        out_shape=[
            jax.ShapeDtypeStruct((total, 2, rows, LANES), f32),
            jax.ShapeDtypeStruct((n_kz, 3, rows, ny), f32),
            jax.ShapeDtypeStruct((n_kz, 2, per_group, rows, ny), f32),
            jax.ShapeDtypeStruct((COIL_GROUPS,) + times.shape, f32),
            jax.ShapeDtypeStruct((COIL_GROUPS,) + sampling_mask.shape, jnp.int32),
        ],
        in_specs=[vmem, vmem, any_, any_, any_, any_],
        out_specs=[any_] * 5,
        scratch_shapes=[
            pltpu.VMEM((n_kz, COIL_GROUPS, 2, rows, LANES), f32),
            dma((total,)), dma((total,)),
            dma((n_kz,)), dma((n_kz,)), dma((n_kz,)), dma((n_kz,)),
            dma((COIL_GROUPS,)), dma((COIL_GROUPS,)), dma((COIL_GROUPS,)), dma((COIL_GROUPS,)),
            dma((5,)),
        ],
        compiler_params=pltpu.CompilerParams(
            collective_id=0, has_side_effects=True, vmem_limit_bytes=VMEM_LIMIT
        ),
        name="gather",
    )(direction_maps, direction_coils, point_maps, point_coils, times, sampling_mask)

    y_forward, y_backward = (jnp.asarray(t) for t in tables_y(ny))
    z_forward, z_backward = (jnp.asarray(t) for t in tables_z(nz))

    def whole(array):
        return pl.BlockSpec(array.shape, lambda t: (0,) * array.ndim)

    grads = pl.pallas_call(
        functools.partial(transform_kernel, n_ti, n_kz, per_group, bins),
        out_shape=jax.ShapeDtypeStruct((total, 2, rows, LANES), f32),
        grid=(bins,),
        in_specs=[
            whole(got_dir), whole(got_maps), whole(got_coils),
            pl.BlockSpec((1, 1, 8, LANES), lambda t: (t // local_bins, t % local_bins, 0, 0)),
            pl.BlockSpec((1, 1, nz, ny), lambda t: (t // local_bins, t % local_bins, 0, 0)),
            whole(y_forward), whole(y_backward), whole(z_forward), whole(z_backward),
        ],
        out_specs=pl.BlockSpec((total, 2, rows, LANES), lambda t: (0, 0, 0, 0)),
        scratch_shapes=[
            pltpu.VMEM((3, nz, ny), f32),
            pltpu.VMEM((2 * per_group, nz, ny), f32),
            pltpu.VMEM((3, nz, ny), f32),
            pltpu.VMEM((2 * per_group, nz, ny), f32),
            pltpu.VMEM((3, nz, ny), f32),
            pltpu.VMEM((2 * per_group, nz, ny), f32),
        ],
        compiler_params=pltpu.CompilerParams(vmem_limit_bytes=VMEM_LIMIT),
        name="transform",
    )(got_dir, got_maps, got_coils, got_times, got_mask, y_forward, y_backward, z_forward, z_backward)

    packed = (n_kz, COIL_GROUPS + 1, rows, LANES)
    return tuple(pl.pallas_call(
        functools.partial(update_kernel, n_ti, n_kz, per_group),
        out_shape=[
            jax.ShapeDtypeStruct(a.shape, f32)
            for a in (residual_maps, residual_coils, direction_maps, direction_coils)
        ],
        in_specs=[any_, vmem, vmem, vmem, vmem],
        out_specs=[vmem] * 4,
        scratch_shapes=[
            pltpu.VMEM((total, 2, rows, LANES), f32),
            pltpu.VMEM(packed, f32), pltpu.VMEM(packed, f32), pltpu.VMEM(packed, f32),
            pltpu.VMEM((8, LANES), f32), pltpu.VMEM((total, 8, LANES), f32),
            dma((total,)), dma((total,)), dma((total,)), dma((total,)), dma((1,)),
        ],
        compiler_params=pltpu.CompilerParams(
            collective_id=1, has_side_effects=True, vmem_limit_bytes=VMEM_LIMIT
        ),
        name="update",
    )(grads, direction_maps, direction_coils, residual_maps, residual_coils))


def solution(mesh):
    in_specs = (
        P(None, None, "kz", None),
        P(None, None, None, "kz", None),
        P(None, None, "kz", "ti"),
        P(None, None, None, "kz", "ti"),
        P(None, None, "kz", "ti"),
        P(None, None, None, "kz", "ti"),
        P("ti"),
        P("ti", None, None),
    )
    out_specs = (
        P(None, None, "kz", "ti"),
        P(None, None, None, "kz", "ti"),
        P(None, None, "kz", "ti"),
        P(None, None, None, "kz", "ti"),
    )
    body = functools.partial(shards, mesh.shape["ti"], mesh.shape["kz"])
    return jax.shard_map(body, mesh=mesh, in_specs=in_specs, out_specs=out_specs, check_vma=False)
```

time: 614 us -> 133 us (0.22)
  waiting for transfers between devices: 324 us -> 0 us
  blocking collectives: 127 us -> 0 us
  Pallas kernels: 0 us -> 116 us
  matrix products: 54.1 us -> 0 us
  local copies, waits for them, and re-layouts: 44.6 us -> 15.7 us
  other arithmetic: 28.7 us -> 0 us
  between operations: 21.4 us -> 0.79 us
  starting transfers between devices: 10.7 us -> 0 us
    psum x1 -> x0, waiting for transfers between devices: 119 us -> none  [shards(): total_maps, total_coils = lax.psum((grad_maps, grad_coils), 'ti')]
    pallas_call x0 -> x3, Pallas kernels: none -> 116 us  [the longest x1 48 us: shards(): pl.pallas_call(functools.partial(update_kernel, n_ti, n_kz, per_group), o...]
    all_to_all x2 -> x0, waiting for transfers between devices: 114 us -> none  [the longest x1 59.3 us: shards(): lax.all_to_all(images, 'kz', split_axis=3, concat_axis=4, tiled=True)]
    all_gather x1 -> x0, waiting for transfers between devices: 89.2 us -> none  [shards(): lax.all_gather(direction_coils, 'ti', axis=4, tiled=True)]
    psum x2 -> x0, blocking collectives: 79.3 us -> none  [the longest x1 40.4 us: shards(): new_norm = lax.psum(inner_sum(updated, updated), ('ti', 'kz'))]
    dot_general x16 -> x0, matrix products: 54.1 us -> none  [the longest x8 26.6 us: contract(): jnp.einsum('kz,...zy->...ky', matrix, values, precision=lax.Precision.HIG...]
    all_gather x1 -> x0, blocking collectives: 47.7 us -> none  [shards(): lax.all_gather(direction_maps, 'ti', axis=3, tiled=True)]
    mul x7 -> x0, local copies, waits for them, and re-layouts: 19.1 us -> none  [the longest x2 11.4 us: shards(): full_coils[0][None] * signal[:, None]]
  transfers between devices with their start and end apart: 4 -> 0, of which waited for: 4 -> 0; matrix products, arithmetic and copies ran while one was open for 3% -> 0% of each run, Pallas kernels for 0% -> 0%
where the time goes in v1:
time: 133 us
  Pallas kernels  116 us (87%)
  local copies, waits for them, and re-layouts  15.7 us (12%)
    pallas_call x1, Pallas kernels, shards(): pl.pallas_call(functools.partial(update_kernel, n_ti, n_kz, per_group), o...  48 us
    pallas_call x1, Pallas kernels, shards(): pl.pallas_call(functools.partial(gather_kernel, n_ti, n_kz, per_group), o...  44.1 us
    pallas_call x1, Pallas kernels, shards(): pl.pallas_call(functools.partial(transform_kernel, n_ti, n_kz, per_group,...  24.2 us
    unnamed x36, local copies, waits for them, and re-layouts  9.83 us
    pallas_call x4, local copies, waits for them, and re-layouts, shards(): pl.pallas_call(functools.partial(update_kernel, n_ti, n_kz, per_group), o...  5.77 us

profile of v1, /device:TPU:0, one launch (start us, length us, event | category | flops | bytes accessed | tf_op | source)
XLA Modules:
  0.0 132.7 jit_solution(13690071753063793344)
XLA Ops:
  0.6 0.0 copy-start.13
  0.6 0.0 copy-start.15
  0.7 0.0 copy-start.7
  0.7 0.0 copy-start.10
  0.7 1.7 %copy.17.dir_coils = f32[2,8,4,40,32]{4,3,2,1,0:T(8,128)S(1)} copy(f32[2,8,4,40,32]{3,4,2,1,0:T(8,128)} %param.15) | data formatting | bytes 655360 | tf_op args[3]
  2.4 0.0 copy-done.13
  2.4 0.1 copy.16.dir_maps
  2.6 0.0 copy-done.15
  2.6 0.1 broadcast_in_dim.2.times
  2.6 0.0 copy-done.7
  2.6 0.0 copy-done.10
  2.6 0.0 copy-start.5
  2.6 0.0 copy-start.6
  2.7 0.0 copy-start.8
  2.7 0.0 copy-start.9
  2.7 44.1 %gather.1 = (f32[32,2,40,128]{3,2,1,0:T(8,128)S(1)}, f32[4,3,40,256]{3,2,1,0:T(8,128)S(1)}, f32[4,2,2,40,256]{4,3,2,1,0:T(8,128)S(1)}, f32[4,2,8,128]{3,2,1,0:T(8,128)S(1)}, s32[4,2,160,256]{3,2,1,0:T(8,128)S(1)}) custom-call(f32[3,4,40,32]{3,2,1,0:T(8,128)S(1)} %copy.16.dir_maps, f32[2,8,4,40,32]{4,3,2,1,0:T(8,128)S(1)} %copy.17.dir_coils, ...), custom_call_target="tpu_custom_call" | custom-call | tf_op jit(solution)/shard_map/gather/pallas_call | solution.py:428
  46.8 0.0 copy-start
  46.8 1.1 copy-done
  47.9 0.0 copy-start.1
  47.9 1.1 copy-done.1
  49.0 0.0 copy-done.5
  49.0 0.0 copy-done.6
  49.0 0.0 copy-done.8
  49.0 0.0 copy-done.9
  49.0 24.2 %transform.1.grads = f32[32,2,40,128]{3,2,1,0:T(8,128)S(1)} custom-call(f32[32,2,40,128]{3,2,1,0:T(8,128)} %copy-done, f32[4,3,40,256]{3,2,1,0:T(8,128)S(1)} %get-tuple-element.10.got_maps, f32[4,2,2,40,256]{4,3,2,1,0:T(8,128)S(1)} %get-tuple-element.11.got_coils, f32[4,2,8,128]{3,2,1,0:T(8,128)S(1)} %get-tuple-element.12.times, ...), custom_call_target="tpu_custom_call" | custom-call | tf_op jit(solution)/shard_map/transform/pallas_call | solution.py:458
  73.2 0.0 copy-start.14
  73.2 2.8 %copy.21.res_coils = f32[2,8,4,40,32]{4,3,2,1,0:T(8,128)} copy(f32[2,8,4,40,32]{3,4,2,1,0:T(8,128)} %param.17) | data formatting | bytes 655360 | tf_op args[5]
  76.0 0.0 copy-done.14
  76.0 0.1 copy.20.res_maps
  76.1 48.0 %update.1 = (f32[3,4,40,32]{3,2,1,0:T(8,128)S(1)}, f32[2,8,4,40,32]{4,3,2,1,0:T(8,128)S(1)}, f32[3,4,40,32]{3,2,1,0:T(8,128)S(1)}, f32[2,8,4,40,32]{4,3,2,1,0:T(8,128)S(1)}) custom-call(f32[32,2,40,128]{3,2,1,0:T(8,128)S(1)} %transform.1.grads, f32[3,4,40,32]{3,2,1,0:T(8,128)S(1)} %copy.16.dir_maps, f32[2,8,4,40,32]{4,3,2,1,0:T(8,128)S(1)} %copy.17.dir_coils, ...), custom_call_target="tpu_custom_call" | custom-call | tf_op jit(solution)/shard_map/update/pallas_call | solution.py:482
  124.1 0.0 copy-start.2
  124.1 1.1 copy-done.2
  125.2 0.0 copy-start.4
  125.2 1.1 copy-done.4
  126.2 0.0 copy-start.11
  126.2 0.7 copy-done.11
  127.0 0.0 copy-start.3
  127.0 2.8 %copy.23 = f32[2,8,4,40,32]{3,4,2,1,0:T(8,128)} copy(f32[2,8,4,40,32]{4,3,2,1,0:T(8,128)} %copy-done.4) | data formatting | bytes 655360 | tf_op jit(solution)/shard_map/update/pallas_call | solution.py:482
  129.7 0.0 copy-start.12
  129.8 0.0 copy-done.3
  129.8 1.4 %copy.25 = f32[2,8,4,40,32]{3,4,2,1,0:T(8,128)} copy(f32[2,8,4,40,32]{4,3,2,1,0:T(8,128)S(1)} %copy-done.3) | data formatting | bytes 655360 | tf_op jit(solution)/shard_map/update/pallas_call | solution.py:482
  131.1 0.0 copy-done.12
  131.1 0.8 copy.22
  131.9 0.8 copy.24
Async XLA Ops:
  0.6 1.8 %copy-start.13 = (f32[3,4,40,32]{2,3,1,0:T(8,128)S(1)}, f32[3,4,40,32]{2,3,1,0:T(8,128)}, u32[]{:S(2)}) copy-start(f32[3,4,40,32]{2,3,1,0:T(8,128)} %param.14) | copy-start | bytes 184324
  0.6 1.9 %copy-start.15 = (f32[2]{0:T(128)S(1)}, f32[2]{0:T(128)}, u32[]{:S(2)}) copy-start(f32[2]{0:T(128)} %param.18) | copy-start | bytes 28
  0.7 2.0 %copy-start.7 = (f32[3,4,40,256]{3,2,1,0:T(8,128)S(1)}, f32[3,4,40,256]{3,2,1,0:T(8,128)}, u32[]{:S(2)}) copy-start(f32[3,4,40,256]{3,2,1,0:T(8,128)} %maps.1) | copy-start | bytes 1474564
  0.7 2.0 %copy-start.10 = (s32[2,160,256]{2,1,0:T(8,128)S(1)}, s32[2,160,256]{2,1,0:T(8,128)}, u32[]{:S(2)}) copy-start(s32[2,160,256]{2,1,0:T(8,128)} %mask.1) | copy-start | bytes 983044
  2.6 46.3 %copy-start.5 = (bf16[2,512,512]{2,1,0:T(8,128)(2,1)S(1)}, bf16[2,512,512]{2,1,0:T(8,128)(2,1)}, u32[]{:S(2)}) copy-start(bf16[2,512,512]{2,1,0:T(8,128)(2,1)} %constant.8.clone.y_forward) | copy-start | bytes 3145732
  2.6 46.3 %copy-start.6 = (bf16[2,512,512]{2,1,0:T(8,128)(2,1)S(1)}, bf16[2,512,512]{2,1,0:T(8,128)(2,1)}, u32[]{:S(2)}) copy-start(bf16[2,512,512]{2,1,0:T(8,128)(2,1)} %constant.9.clone.y_backward) | copy-start | bytes 3145732
  2.7 46.3 %copy-start.8 = (bf16[2,320,320]{2,1,0:T(8,128)(2,1)S(1)}, bf16[2,320,320]{2,1,0:T(8,128)(2,1)}, u32[]{:S(2)}) copy-start(bf16[2,320,320]{2,1,0:T(8,128)(2,1)} %constant.10.clone.z_forward) | copy-start | bytes 1228804
  2.7 46.3 %copy-start.9 = (bf16[2,320,320]{2,1,0:T(8,128)(2,1)S(1)}, bf16[2,320,320]{2,1,0:T(8,128)(2,1)}, u32[]{:S(2)}) copy-start(bf16[2,320,320]{2,1,0:T(8,128)(2,1)} %constant.11.clone.z_backward) | copy-start | bytes 1228804
  46.8 1.1 copy-start
  47.9 1.1 copy-start.1
  73.2 2.8 %copy-start.14 = (f32[3,4,40,32]{2,3,1,0:T(8,128)S(1)}, f32[3,4,40,32]{2,3,1,0:T(8,128)}, u32[]{:S(2)}) copy-start(f32[3,4,40,32]{2,3,1,0:T(8,128)} %param.16) | copy-start | bytes 184324
  124.1 1.1 copy-start.2
  125.2 1.1 copy-start.4
  126.2 0.7 copy-start.11
  127.0 2.8 %copy-start.3 = (f32[2,8,4,40,32]{4,3,2,1,0:T(8,128)S(1)}, f32[2,8,4,40,32]{4,3,2,1,0:T(8,128)}, u32[]{:S(2)}) copy-start(f32[2,8,4,40,32]{4,3,2,1,0:T(8,128)} %copy-done.2) | copy-start | bytes 983044
  129.7 1.4 %copy-start.12 = (f32[3,4,40,32]{3,2,1,0:T(8,128)S(1)}, f32[3,4,40,32]{3,2,1,0:T(8,128)}, u32[]{:S(2)}) copy-start(f32[3,4,40,32]{3,2,1,0:T(8,128)} %copy-done.11) | copy-start | bytes 184324

commit v2 on v0

v2 whole, which is shorter than its diff:
```python
import functools
import math

import jax
import jax.numpy as jnp
import ml_dtypes
import numpy as np
from jax import lax
from jax.experimental import pallas as pl
from jax.experimental.pallas import tpu as pltpu
from jax.sharding import PartitionSpec as P

MESH = pl.DeviceIdType.MESH
regular_weight = 2.0
COIL_GROUPS = 4
LANES = 128
VMEM_LIMIT = 48 * 1024 * 1024


def split_table(table):
    high = table.astype(ml_dtypes.bfloat16)
    low = (table - high.astype(np.float64)).astype(ml_dtypes.bfloat16)
    return np.stack([high, low])


def dft_parts(length):
    indices = np.arange(length)
    angles = (indices[:, None] * indices[None, :] % length) * (2.0 * math.pi / length)
    factor = 1.0 / math.sqrt(length)
    return np.cos(angles) * factor, np.sin(angles) * factor


def tables_y(length):
    c, s = dft_parts(length)
    forward = np.block([[c, -s], [s, c]])
    backward = np.block([[c, s], [-s, c]])
    return split_table(forward), split_table(backward)


def tables_z(length):
    c, s = dft_parts(length)
    forward = np.block([[c, s], [-s, c]])
    backward = np.block([[c, -s], [s, c]])
    return split_table(forward), split_table(backward)


def halves(values):
    high = values.astype(jnp.bfloat16)
    low = (values - high.astype(jnp.float32)).astype(jnp.bfloat16)
    return high, low


dot = functools.partial(jnp.dot, preferred_element_type=jnp.float32)


def from_right(values, table):
    high, low = halves(values)
    return dot(high, table[0]) + (dot(low, table[0]) + dot(high, table[1]))


def from_left(table, values):
    high, low = halves(values)
    return dot(table[0], high) + (dot(table[0], low) + dot(table[1], high))


def lane_spans(rows, planes, width):
    count = LANES // (planes * width)
    chunk = -(-(-(-rows // count)) // 8) * 8
    return chunk, [(start, min(chunk, rows - start)) for start in range(0, rows, chunk)]


def lane_blocks(rows, width):
    return lax.broadcasted_iota(jnp.int32, (rows, LANES), 1) // width


def turned(values, shift):
    shift %= LANES
    return pltpu.roll(values, shift, 1) if shift else values


def tall(values, rows):
    missing = rows - values.shape[0]
    if missing:
        values = jnp.concatenate([values, jnp.zeros((missing,) + values.shape[1:], values.dtype)], axis=0)
    return values


def fold(parts, width):
    rows = parts[0].shape[1]
    planes = len(parts)
    chunk, spans = lane_spans(rows, planes, width)
    block = tall(jnp.concatenate(parts, axis=0), LANES).T
    if len(spans) == 1:
        return tall(block, chunk)
    ids = lane_blocks(chunk, planes * width)
    value = jnp.zeros((chunk, LANES), jnp.float32)
    for i, (start, size) in enumerate(spans):
        moved = turned(tall(block[start : start + size], chunk), i * planes * width)
        value = jnp.where(ids == i, moved, value)
    return value


def unfold(block, planes, rows, width):
    _, spans = lane_spans(rows, planes, width)
    parts = [turned(block[:size], -i * planes * width) for i, (_, size) in enumerate(spans)]
    return (jnp.concatenate(parts, axis=0) if len(parts) > 1 else parts[0]).T


def scatter_lanes(blocks, planes, rows, width, store):
    _, spans = lane_spans(rows, planes, width)
    for p in range(planes):
        for i, (start, size) in enumerate(spans):
            ids = lane_blocks(size, width)
            value = None
            for j, block in enumerate(blocks):
                moved = turned(block[:size], (j - i * planes - p) * width)
                value = moved if value is None else jnp.where(ids == j, moved, value)
            store(p, slice(start, start + size), value)


def collect_lanes(planes, j, rows, width):
    chunk, spans = lane_spans(rows, len(planes), width)
    ids = lane_blocks(chunk, width)
    value = jnp.zeros((chunk, LANES), jnp.float32)
    for p, plane in enumerate(planes):
        for i, (start, size) in enumerate(spans):
            q = i * len(planes) + p
            moved = turned(tall(plane[start : start + size], chunk), (q - j) * width)
            value = jnp.where(ids == q, moved, value)
    return value


def step_kernel(
    n_ti, n_kz, per_group, four, one, two,
    dir_maps, dir_coils, res_maps, res_coils, maps, coils, times, mask, tables_y_in, tables_z_in,
    new_res_maps, new_res_coils, new_dir_maps, new_dir_coils,
    send_a, send_b, got_a, got_b, got_maps, got_coils, got_times, got_mask, ytab, ztab,
    p_maps, p_coils, s_maps, s_coils, g_maps, g_coils,
    back_a, back_b, ret_a, ret_b, app_maps, app_coils, sums, got_sums,
    a_out, a_in, b_out, b_in, ra_out, ra_in, rb_out, rb_in, sum_out, sum_in,
    map_out, map_in, coil_out, coil_in, time_out, time_in, mask_out, mask_in, pair_out, pair_in, own,
):
    total = n_ti * n_kz
    ti = lax.axis_index("ti")
    kz = lax.axis_index("kz")
    me = ti * n_kz + kz
    group = lax.rem(ti, COIL_GROUPS)
    first = (ti // COIL_GROUPS) * COIL_GROUPS
    core = lax.rem(kz, 2)
    pair = kz + 1 - 2 * core
    width = dir_maps.shape[2]
    rows = dir_maps.shape[3]
    nz, ny = mask.shape[1:]
    tiles = ny // LANES
    per_tile = LANES // width
    my_coils = pl.ds(group * per_group, per_group)

    barrier = pltpu.get_barrier_semaphore()

    def greet(offset, carry):
        other = lax.rem(me + offset, total)
        pl.semaphore_signal(
            barrier, inc=1, device_id=(other // n_kz, lax.rem(other, n_kz)), device_id_type=MESH
        )
        return carry

    lax.fori_loop(1, total, greet, 0)

    locals_ = [
        pltpu.make_async_copy(maps.at[:, kz], got_maps.at[kz], own.at[0]),
        pltpu.make_async_copy(coils.at[:, my_coils, kz], got_coils.at[kz], own.at[1]),
        pltpu.make_async_copy(times, got_times.at[group], own.at[2]),
        pltpu.make_async_copy(mask, got_mask.at[group], own.at[3]),
        pltpu.make_async_copy(tables_y_in, ytab, own.at[4]),
        pltpu.make_async_copy(tables_z_in, ztab, own.at[5]),
    ]
    for copy in locals_:
        copy.start()

    for x in range(n_kz):
        last = fold([dir_maps[2, x]], width)
        for g in range(COIL_GROUPS):
            c = g * per_group
            send_a[x, g, :four] = fold([dir_coils[0, c, x], dir_coils[1, c, x], dir_maps[0, x], dir_maps[1, x]], width)
            send_a[x, g, four:] = last
            send_b[x, g] = fold([dir_coils[0, c + 1, x], dir_coils[1, c + 1, x]], width)
    got_a[me] = send_a[kz, group]
    got_b[me] = send_b[kz, group]

    pl.semaphore_wait(barrier, total - 1)

    def remote(src, dst, out_sem, in_sem, where):
        return pltpu.make_async_remote_copy(src, dst, out_sem, in_sem, device_id=where, device_id_type=MESH)

    def split_id(other):
        return other // n_kz, lax.rem(other, n_kz)

    def a_copy(other, slot):
        t, k = split_id(other)
        return remote(send_a.at[k, lax.rem(t, COIL_GROUPS)], got_a.at[slot], a_out.at[other], a_in.at[slot], (t, k))

    def b_copy(other, slot):
        t, k = split_id(other)
        return remote(send_b.at[k, lax.rem(t, COIL_GROUPS)], got_b.at[slot], b_out.at[other], b_in.at[slot], (t, k))

    def ra_copy(other, slot):
        return remote(back_a.at[other], ret_a.at[slot], ra_out.at[other], ra_in.at[slot], split_id(other))

    def rb_copy(other, slot):
        return remote(back_b.at[other], ret_b.at[slot], rb_out.at[other], rb_in.at[slot], split_id(other))

    def sum_copy(other, slot):
        return remote(sums, got_sums.at[slot], sum_out.at[other], sum_in.at[slot], split_id(other))

    def send_all(copy):
        def body(offset, carry):
            copy(lax.rem(me + offset, total), me).start()
            return carry

        lax.fori_loop(1, total, body, 0)

    def wait_all(copy):
        def body(offset, carry):
            other = lax.rem(me + offset, total)
            one_copy = copy(other, other)
            one_copy.wait_send()
            one_copy.wait_recv()
            return carry

        lax.fori_loop(1, total, body, 0)

    def point_copies(other, slot):
        return [
            remote(maps.at[:, other], got_maps.at[slot], map_out.at[other], map_in.at[slot], (ti, other)),
            remote(coils.at[:, my_coils, other], got_coils.at[slot], coil_out.at[other], coil_in.at[slot], (ti, other)),
        ]

    def bin_copies(other, slot):
        where = (first + other, kz)
        return [
            remote(times, got_times.at[slot], time_out.at[other], time_in.at[slot], where),
            remote(mask.at[core], got_mask.at[slot, core], mask_out.at[other], mask_in.at[slot], where),
        ]

    def pair_copy(slot, plane):
        where = (ti, pair)
        return remote(got_mask.at[slot, plane], got_mask.at[slot, plane], pair_out.at[slot], pair_in.at[slot], where)

    send_all(a_copy)
    for offset in range(1, n_kz):
        for copy in point_copies(lax.rem(kz + offset, n_kz), kz):
            copy.start()
    for offset in range(1, COIL_GROUPS):
        for copy in bin_copies(lax.rem(group + offset, COIL_GROUPS), group):
            copy.start()
    send_all(b_copy)

    for copy in locals_:
        copy.wait()
    for offset in range(1, n_kz):
        other = lax.rem(kz + offset, n_kz)
        for copy in point_copies(other, other):
            copy.wait_send()
            copy.wait_recv()
    for k in range(n_kz):
        span = slice(k * rows, (k + 1) * rows)
        for m in range(3):
            p_maps[m, span, :] = got_maps[k, m]
        for c in range(per_group):
            for ri in range(2):
                p_coils[2 * c + ri, span, :] = got_coils[k, ri, c]
    wait_all(a_copy)

    def store_to(targets, k, h):
        def store(p, span, value):
            ref, plane = targets[p]
            ref[plane, k * rows + span.start : k * rows + span.stop, h * LANES : (h + 1) * LANES] = value

        return store

    coil_zero = [(s_coils, 0), (s_coils, 1)]
    coil_one = [(s_coils, 2), (s_coils, 3)]
    for k in range(n_kz):
        for h in range(tiles):
            sources = [(h * per_tile + j) * n_kz + k for j in range(per_tile)]
            scatter_lanes(
                [got_a[s, :four] for s in sources], 4, rows, width,
                store_to(coil_zero + [(s_maps, 0), (s_maps, 1)], k, h),
            )
            scatter_lanes([got_a[s, four:] for s in sources], 1, rows, width, store_to([(s_maps, 2)], k, h))

    for offset in range(1, COIL_GROUPS):
        other = lax.rem(group + offset, COIL_GROUPS)
        for copy in bin_copies(other, other):
            copy.wait_send()
            copy.wait_recv()
        pair_copy(other, core).start()

    g_maps[...] = jnp.zeros_like(g_maps)
    g_coils[...] = jnp.zeros_like(g_coils)

    def coil_pass(c):
        def body(offset, carry):
            other = lax.rem(group + offset, COIL_GROUPS)
            if c == 0:
                @pl.when(offset > 0)
                def _():
                    pair_copy(other, core).wait_send()
                    pair_copy(other, 1 - core).wait_recv()

            amplitude = p_maps[1]
            model = []
            rows_in = []
            kept = []
            for b in range(2):
                tau = got_times[other, b, 0:1, 0:1]
                decays = jnp.exp(-tau * p_maps[2])
                signal = p_maps[0] - amplitude * decays
                slope = amplitude * tau * decays
                signal_step = s_maps[0] - s_maps[1] * decays + slope * s_maps[2]
                real = p_coils[2 * c] * signal_step + s_coils[2 * c] * signal
                imag = p_coils[2 * c + 1] * signal_step + s_coils[2 * c + 1] * signal
                rows_in.append(jnp.concatenate([real, imag], axis=1))
                model.append((decays, signal, slope))
                kept.append(got_mask[other, b].astype(jnp.float32))
            both = from_right(jnp.concatenate(rows_in, axis=0), ytab[0])
            along_z = jnp.concatenate(
                [
                    jnp.concatenate([both[b * nz : (b + 1) * nz, :ny], both[b * nz : (b + 1) * nz, ny:]], axis=0)
                    for b in range(2)
                ],
                axis=1,
            )
            kept = jnp.concatenate([jnp.concatenate(kept, axis=1)] * 2, axis=0)
            back = from_left(ztab[1], from_left(ztab[0], along_z) * kept)
            both = jnp.concatenate(
                [
                    jnp.concatenate([back[:nz, b * ny : (b + 1) * ny], back[nz:, b * ny : (b + 1) * ny]], axis=1)
                    for b in range(2)
                ],
                axis=0,
            )
            back = from_right(both, ytab[1])
            for b, (decays, signal, slope) in enumerate(model):
                real = back[b * nz : (b + 1) * nz, :ny]
                imag = back[b * nz : (b + 1) * nz, ny:]
                projected = p_coils[2 * c] * real + p_coils[2 * c + 1] * imag
                g_coils[2 * c] += signal * real
                g_coils[2 * c + 1] += signal * imag
                g_maps[0] += projected
                g_maps[1] -= decays * projected
                g_maps[2] += slope * projected
            return carry

        lax.fori_loop(0, COIL_GROUPS, body, 0)

    coil_pass(0)

    for k in range(n_kz):
        span = slice(k * rows, (k + 1) * rows)
        for h in range(tiles):
            lanes = slice(h * LANES, (h + 1) * LANES)
            planes = [g_coils[p, span, lanes] for p in range(2)]
            for j in range(per_tile):
                back_b[(h * per_tile + j) * n_kz + k] = collect_lanes(planes, j, rows, width)
    send_all(rb_copy)
    ret_b[me] = back_b[me]

    wait_all(b_copy)
    for k in range(n_kz):
        for h in range(tiles):
            sources = [(h * per_tile + j) * n_kz + k for j in range(per_tile)]
            scatter_lanes([got_b[s] for s in sources], 2, rows, width, store_to(coil_one, k, h))

    coil_pass(1)

    for k in range(n_kz):
        span = slice(k * rows, (k + 1) * rows)
        for h in range(tiles):
            lanes = slice(h * LANES, (h + 1) * LANES)
            planes = [g_coils[2, span, lanes], g_coils[3, span, lanes], g_maps[0, span, lanes], g_maps[1, span, lanes]]
            final = [g_maps[2, span, lanes]]
            for j in range(per_tile):
                to = (h * per_tile + j) * n_kz + k
                back_a[to, :four] = collect_lanes(planes, j, rows, width)
                back_a[to, four:] = collect_lanes(final, j, rows, width)
    send_all(ra_copy)
    ret_a[me] = back_a[me]
    wait_all(rb_copy)

    parts = {"old": None, "bend": None, "cross": None, "square": None}

    def settle(applied, grad, d, r):
        a = grad + regular_weight * d
        for key, value in (("old", r * r), ("bend", d * a), ("cross", r * a), ("square", a * a)):
            parts[key] = value if parts[key] is None else parts[key] + value
        return a

    def settle_coils(c, x, flat):
        for ri in range(2):
            grad = flat[ri * width : (ri + 1) * width]
            app_coils[ri, c, x] = settle(None, grad, dir_coils[ri, c, x], res_coils[ri, c, x])

    def added(terms):
        return functools.reduce(lambda u, v: u + v, terms)

    for x in range(n_kz):
        for g in range(COIL_GROUPS):
            block = added([ret_b[t * n_kz + x] for t in range(g, n_ti, COIL_GROUPS)])
            settle_coils(g * per_group, x, unfold(block, 2, rows, width))

    wait_all(ra_copy)
    for x in range(n_kz):
        summed = []
        for g in range(COIL_GROUPS):
            block = added([ret_a[t * n_kz + x, :four] for t in range(g, n_ti, COIL_GROUPS)])
            summed.append(block)
            settle_coils(g * per_group + 1, x, unfold(block, 4, rows, width))
        flat = unfold(added(summed), 4, rows, width)
        final = unfold(added([ret_a[t * n_kz + x, four:] for t in range(n_ti)]), 1, rows, width)
        grads = [flat[2 * width : 3 * width], flat[3 * width : 4 * width], final[:width]]
        for m, grad in enumerate(grads):
            app_maps[m, x] = settle(None, grad, dir_maps[m, x], res_maps[m, x])

    row = lax.broadcasted_iota(jnp.int32, sums.shape, 0)
    tile = jnp.zeros(sums.shape, jnp.float32)
    for i, part in enumerate(parts.values()):
        tile = jnp.where(row == i, jnp.sum(part, keepdims=True), tile)
    sums[...] = tile
    send_all(sum_copy)
    got_sums[me] = tile
    wait_all(sum_copy)
    whole = jnp.sum(got_sums[...], axis=0)
    old, bend, cross, square = (whole[i : i + 1, :rows] for i in range(4))
    step = old / bend
    ratio = (old - 2.0 * step * cross + step * step * square) / old
    for x in range(n_kz):
        for m in range(3):
            r = res_maps[m, x] - step * app_maps[m, x]
            new_res_maps[m, x] = r
            new_dir_maps[m, x] = r + ratio * dir_maps[m, x]
        for c in range(COIL_GROUPS * per_group):
            for ri in range(2):
                r = res_coils[ri, c, x] - step * app_coils[ri, c, x]
                new_res_coils[ri, c, x] = r
                new_dir_coils[ri, c, x] = r + ratio * dir_coils[ri, c, x]


def shards(
    n_ti, n_kz,
    point_maps, point_coils, direction_maps, direction_coils,
    residual_maps, residual_coils, inversion_times, sampling_mask,
):
    total = n_ti * n_kz
    coils = point_coils.shape[1]
    per_group = coils // COIL_GROUPS
    rows, ny = point_maps.shape[2:]
    width = ny // n_ti
    local_bins, nz, _ = sampling_mask.shape
    f32 = jnp.float32
    any_ = pl.BlockSpec(memory_space=pl.ANY)
    vmem = pl.BlockSpec(memory_space=pltpu.VMEM)
    dma = pltpu.SemaphoreType.DMA
    times = jnp.broadcast_to(inversion_times[:, None, None], (local_bins, 8, LANES))
    y_tables = jnp.asarray(np.stack(tables_y(ny)))
    z_tables = jnp.asarray(np.stack(tables_z(nz)))
    flipped = [
        jnp.swapaxes(a, -1, -2) for a in (direction_maps, direction_coils, residual_maps, residual_coils)
    ]
    four, one, two = (lane_spans(rows, planes, width)[0] for planes in (4, 1, 2))
    a_rows = four + one

    outs = pl.pallas_call(
        functools.partial(step_kernel, n_ti, n_kz, per_group, four, one, two),
        out_shape=[jax.ShapeDtypeStruct(flipped[i].shape, f32) for i in (2, 3, 0, 1)],
        in_specs=[vmem] * 4 + [any_] * 6,
        out_specs=[vmem] * 4,
        scratch_shapes=[
            pltpu.VMEM((n_kz, COIL_GROUPS, a_rows, LANES), f32),
            pltpu.VMEM((n_kz, COIL_GROUPS, two, LANES), f32),
            pltpu.VMEM((total, a_rows, LANES), f32),
            pltpu.VMEM((total, two, LANES), f32),
            pltpu.VMEM((n_kz, 3, rows, ny), f32),
            pltpu.VMEM((n_kz, 2, per_group, rows, ny), f32),
            pltpu.VMEM((COIL_GROUPS,) + times.shape, f32),
            pltpu.VMEM((COIL_GROUPS,) + sampling_mask.shape, jnp.int32),
            pltpu.VMEM(y_tables.shape, jnp.bfloat16),
            pltpu.VMEM(z_tables.shape, jnp.bfloat16),
            pltpu.VMEM((3, nz, ny), f32),
            pltpu.VMEM((2 * per_group, nz, ny), f32),
            pltpu.VMEM((3, nz, ny), f32),
            pltpu.VMEM((2 * per_group, nz, ny), f32),
            pltpu.VMEM((3, nz, ny), f32),
            pltpu.VMEM((2 * per_group, nz, ny), f32),
            pltpu.VMEM((total, a_rows, LANES), f32),
            pltpu.VMEM((total, two, LANES), f32),
            pltpu.VMEM((total, a_rows, LANES), f32),
            pltpu.VMEM((total, two, LANES), f32),
            pltpu.VMEM(flipped[0].shape, f32),
            pltpu.VMEM(flipped[1].shape, f32),
            pltpu.VMEM((8, LANES), f32),
            pltpu.VMEM((total, 8, LANES), f32),
        ]
        + [dma((total,))] * 10
        + [dma((n_kz,))] * 4
        + [dma((COIL_GROUPS,))] * 6
        + [dma((6,))],
        compiler_params=pltpu.CompilerParams(
            collective_id=0, has_side_effects=True, vmem_limit_bytes=VMEM_LIMIT
        ),
        name="step",
    )(*flipped, point_maps, point_coils, times, sampling_mask, y_tables, z_tables)
    return tuple(jnp.swapaxes(a, -1, -2) for a in outs)


def solution(mesh):
    in_specs = (
        P(None, None, "kz", None),
        P(None, None, None, "kz", None),
        P(None, None, "kz", "ti"),
        P(None, None, None, "kz", "ti"),
        P(None, None, "kz", "ti"),
        P(None, None, None, "kz", "ti"),
        P("ti"),
        P("ti", None, None),
    )
    out_specs = (
        P(None, None, "kz", "ti"),
        P(None, None, None, "kz", "ti"),
        P(None, None, "kz", "ti"),
        P(None, None, None, "kz", "ti"),
    )
    body = functools.partial(shards, mesh.shape["ti"], mesh.shape["kz"])
    return jax.shard_map(body, mesh=mesh, in_specs=in_specs, out_specs=out_specs, check_vma=False)
```

time: 614 us -> 103 us (0.17)
  waiting for transfers between devices: 324 us -> 0 us
  blocking collectives: 127 us -> 0 us
  Pallas kernels: 0 us -> 91.6 us
  matrix products: 54.1 us -> 0 us
  local copies, waits for them, and re-layouts: 44.6 us -> 10.3 us
  other arithmetic: 28.7 us -> 0 us
  between operations: 21.4 us -> 0.65 us
  starting transfers between devices: 10.7 us -> 0 us
    psum x1 -> x0, waiting for transfers between devices: 119 us -> none  [shards(): total_maps, total_coils = lax.psum((grad_maps, grad_coils), 'ti')]
    all_to_all x2 -> x0, waiting for transfers between devices: 114 us -> none  [the longest x1 59.3 us: shards(): lax.all_to_all(images, 'kz', split_axis=3, concat_axis=4, tiled=True)]
    pallas_call x0 -> x1, Pallas kernels: none -> 91.6 us  [shards(): pl.pallas_call(functools.partial(step_kernel, n_ti, n_kz, per_group, four...]
    all_gather x1 -> x0, waiting for transfers between devices: 89.2 us -> none  [shards(): lax.all_gather(direction_coils, 'ti', axis=4, tiled=True)]
    psum x2 -> x0, blocking collectives: 79.3 us -> none  [the longest x1 40.4 us: shards(): new_norm = lax.psum(inner_sum(updated, updated), ('ti', 'kz'))]
    dot_general x16 -> x0, matrix products: 54.1 us -> none  [the longest x8 26.6 us: contract(): jnp.einsum('kz,...zy->...ky', matrix, values, precision=lax.Precision.HIG...]
    all_gather x1 -> x0, blocking collectives: 47.7 us -> none  [shards(): lax.all_gather(direction_maps, 'ti', axis=3, tiled=True)]
    mul x7 -> x0, local copies, waits for them, and re-layouts: 19.1 us -> none  [the longest x2 11.4 us: shards(): full_coils[0][None] * signal[:, None]]
  transfers between devices with their start and end apart: 4 -> 0, of which waited for: 4 -> 0; matrix products, arithmetic and copies ran while one was open for 3% -> 0% of each run, Pallas kernels for 0% -> 0%
where the time goes in v2:
time: 103 us
  Pallas kernels  91.6 us (89%)
  local copies, waits for them, and re-layouts  10.3 us (10%)
    pallas_call x1, Pallas kernels, shards(): pl.pallas_call(functools.partial(step_kernel, n_ti, n_kz, per_group, four...  91.6 us
    unnamed x16, local copies, waits for them, and re-layouts  9.58 us

profile of v2, /device:TPU:0, one launch (start us, length us, event | category | flops | bytes accessed | tf_op | source)
XLA Modules:
  0.0 102.5 jit_solution(11822885773747732543)
XLA Ops:
  0.6 0.7 broadcast_in_dim.2.times
  1.4 0.0 copy-start
  1.4 1.2 %copy-done = f32[2,8,4,40,32]{3,4,2,1,0:T(8,128)S(1)} copy-done((f32[2,8,4,40,32]{3,4,2,1,0:T(8,128)S(1)}, f32[2,8,4,40,32]{3,4,2,1,0:T(8,128)}, u32[]{:S(2)}) %copy-start) | copy-done | bytes 327704
  2.6 0.0 copy-start.1
  2.6 1.2 %copy-done.1 = bf16[2,2,320,320]{3,2,1,0:T(8,128)(2,1)S(1)} copy-done((bf16[2,2,320,320]{3,2,1,0:T(8,128)(2,1)S(1)}, bf16[2,2,320,320]{3,2,1,0:T(8,128)(2,1)}, u32[]{:S(2)}) %copy-start.1) | copy-done | bytes 819224
  3.8 0.0 copy-start.2
  3.8 1.0 %copy-done.2 = f32[3,4,40,256]{3,2,1,0:T(8,128)S(1)} copy-done((f32[3,4,40,256]{3,2,1,0:T(8,128)S(1)}, f32[3,4,40,256]{3,2,1,0:T(8,128)}, u32[]{:S(2)}) %copy-start.2) | copy-done | bytes 491544
  4.8 0.0 copy-start.3
  4.8 1.0 copy-done.3
  5.8 0.0 copy-start.4
  5.8 0.9 copy-done.4
  6.7 0.0 copy-start.5
  6.7 0.9 copy-done.5
  7.6 91.6 %step.1 = (f32[3,4,32,40]{3,2,1,0:T(8,128)S(1)}, f32[2,8,4,32,40]{4,3,2,1,0:T(8,128)S(1)}, f32[3,4,32,40]{3,2,1,0:T(8,128)S(1)}, f32[2,8,4,32,40]{4,3,2,1,0:T(8,128)S(1)}) custom-call(f32[3,4,32,40]{3,2,1,0:T(8,128)S(1)} %bitcast.13, f32[2,8,4,32,40]{4,3,2,1,0:T(8,128)S(1)} %bitcast.8, f32[3,4,32,40]{3,2,1,0:T(8,128)S(1)} %bitcast.14, ...), custom_call_target="tpu_custom_call" | custom-call | tf_op jit(solution)/shard_map/step/pallas_call | solution.py:473
  99.2 0.7 copy.18
  99.9 1.0 copy.19
  100.9 0.7 copy.20
  101.5 1.0 copy.21
Async XLA Ops:
  1.4 1.2 %copy-start = (f32[2,8,4,40,32]{3,4,2,1,0:T(8,128)S(1)}, f32[2,8,4,40,32]{3,4,2,1,0:T(8,128)}, u32[]{:S(2)}) copy-start(f32[2,8,4,40,32]{3,4,2,1,0:T(8,128)} %param.13) | copy-start | bytes 983044
  2.6 1.2 %copy-start.1 = (bf16[2,2,320,320]{3,2,1,0:T(8,128)(2,1)S(1)}, bf16[2,2,320,320]{3,2,1,0:T(8,128)(2,1)}, u32[]{:S(2)}) copy-start(bf16[2,2,320,320]{3,2,1,0:T(8,128)(2,1)} %constant.5.clone.tables_z_in) | copy-start | bytes 2457604
  3.8 1.0 %copy-start.2 = (f32[3,4,40,256]{3,2,1,0:T(8,128)S(1)}, f32[3,4,40,256]{3,2,1,0:T(8,128)}, u32[]{:S(2)}) copy-start(f32[3,4,40,256]{3,2,1,0:T(8,128)} %maps.1) | copy-start | bytes 1474564
  4.8 1.0 copy-start.3
  5.8 0.9 copy-start.4
  6.7 0.9 copy-start.5

commit v3 on v2

--- a/solution.py
+++ b/solution.py
@@ -3,7 +3,6 @@
 
 import jax
 import jax.numpy as jnp
-import ml_dtypes
 import numpy as np
 from jax import lax
 from jax.experimental import pallas as pl
@@ -14,34 +13,40 @@
 regular_weight = 2.0
 COIL_GROUPS = 4
 LANES = 128
-VMEM_LIMIT = 48 * 1024 * 1024
-
-
-def split_table(table):
-    high = table.astype(ml_dtypes.bfloat16)
-    low = (table - high.astype(np.float64)).astype(ml_dtypes.bfloat16)
-    return np.stack([high, low])
-
-
-def dft_parts(length):
-    indices = np.arange(length)
-    angles = (indices[:, None] * indices[None, :] % length) * (2.0 * math.pi / length)
+VMEM_LIMIT = 60 * 1024 * 1024
+
+
+def half_parts(length, parity):
+    points = np.arange(length // 2)
+    orders = 2 * points + parity
+    angles = (points[:, None] * orders[None, :] % length) * (2.0 * math.pi / length)
     factor = 1.0 / math.sqrt(length)
     return np.cos(angles) * factor, np.sin(angles) * factor
 
 
 def tables_y(length):
-    c, s = dft_parts(length)
-    forward = np.block([[c, -s], [s, c]])
-    backward = np.block([[c, s], [-s, c]])
-    return split_table(forward), split_table(backward)
+    forward, backward = [], []
+    for parity in range(2):
+        c, s = half_parts(length, parity)
+        forward.append(np.block([[c, -s], [s, c]]))
+        backward.append(np.block([[c.T, s.T], [-s.T, c.T]]))
+    return np.stack([np.stack(forward), np.stack(backward)]).astype(np.float32)
 
 
 def tables_z(length):
-    c, s = dft_parts(length)
-    forward = np.block([[c, s], [-s, c]])
-    backward = np.block([[c, -s], [s, c]])
-    return split_table(forward), split_table(backward)
+    forward, backward = [], []
+    for parity in range(2):
+        c, s = half_parts(length, parity)
+        forward.append(np.block([[c.T, s.T], [-s.T, c.T]]))
+        backward.append(np.block([[c, -s], [s, c]]))
+    return np.stack([np.stack(forward), np.stack(backward)]).astype(np.float32)
+
+
+def even_then_odd(length, source_axis):
+    source = lax.broadcasted_iota(jnp.int32, (length, length), source_axis)
+    place = lax.broadcasted_iota(jnp.int32, (length, length), 1 - source_axis)
+    wanted = jnp.where(place < length // 2, 2 * place, 2 * place - length + 1)
+    return jnp.where(source == wanted, 1.0, 0.0).astype(jnp.bfloat16)
 
 
 def halves(values):
@@ -60,7 +65,9 @@
 
 def from_left(table, values):
     high, low = halves(values)
-    return dot(table[0], high) + (dot(table[0], low) + dot(table[1], high))
+    size = table.shape[1]
+    both = dot(table, high)
+    return both[:size] + (both[size:] + dot(table[:size], low))
 
 
 def lane_spans(rows, planes, width):
@@ -132,11 +139,13 @@
 
 def step_kernel(
     n_ti, n_kz, per_group, four, one, two,
-    dir_maps, dir_coils, res_maps, res_coils, maps, coils, times, mask, tables_y_in, tables_z_in,
-    new_res_maps, new_res_coils, new_dir_maps, new_dir_coils,
+    dir_maps_in, dir_coils_in, res_maps_in, res_coils_in, maps, coils, bin_times, mask,
+    tables_y_in, tables_z_in,
+    app_maps, app_coils, scales,
+    dir_maps, dir_coils, res_maps, res_coils, times, order_y, order_z, kept_masks, wide_y, wide_z,
     send_a, send_b, got_a, got_b, got_maps, got_coils, got_times, got_mask, ytab, ztab,
     p_maps, p_coils, s_maps, s_coils, g_maps, g_coils,
-    back_a, back_b, ret_a, ret_b, app_maps, app_coils, sums, got_sums,
+    back_a, back_b, ret_a, ret_b, sums, got_sums,
     a_out, a_in, b_out, b_in, ra_out, ra_in, rb_out, rb_in, sum_out, sum_in,
     map_out, map_in, coil_out, coil_in, time_out, time_in, mask_out, mask_in, pair_out, pair_in, own,
 ):
@@ -155,6 +164,13 @@
     per_tile = LANES // width
     my_coils = pl.ds(group * per_group, per_group)
 
+    early = [
+        pltpu.make_async_copy(dir_maps_in, dir_maps, own.at[6]),
+        pltpu.make_async_copy(dir_coils_in, dir_coils, own.at[7]),
+    ]
+    for copy in early:
+        copy.start()
+
     barrier = pltpu.get_barrier_semaphore()
 
     def greet(offset, carry):
@@ -169,13 +185,19 @@
     locals_ = [
         pltpu.make_async_copy(maps.at[:, kz], got_maps.at[kz], own.at[0]),
         pltpu.make_async_copy(coils.at[:, my_coils, kz], got_coils.at[kz], own.at[1]),
-        pltpu.make_async_copy(times, got_times.at[group], own.at[2]),
         pltpu.make_async_copy(mask, got_mask.at[group], own.at[3]),
-        pltpu.make_async_copy(tables_y_in, ytab, own.at[4]),
-        pltpu.make_async_copy(tables_z_in, ztab, own.at[5]),
+        pltpu.make_async_copy(tables_y_in, wide_y, own.at[4]),
+        pltpu.make_async_copy(tables_z_in, wide_z, own.at[5]),
+        pltpu.make_async_copy(res_maps_in, res_maps, own.at[2]),
+        pltpu.make_async_copy(res_coils_in, res_coils, own.at[8]),
     ]
     for copy in locals_:
         copy.start()
+    for b in range(2):
+        times[b] = jnp.full((8, LANES), bin_times[b], jnp.float32)
+        got_times[group, b] = jnp.full((8, LANES), bin_times[b], jnp.float32)
+    for copy in early:
+        copy.wait()
 
     for x in range(n_kz):
         last = fold([dir_maps[2, x]], width)
@@ -257,6 +279,16 @@
 
     for copy in locals_:
         copy.wait()
+    order_y[...] = even_then_odd(ny, 0)
+    order_z[...] = even_then_odd(nz, 1)
+    for way in range(2):
+        for parity in range(2):
+            high, low = halves(wide_y[way, parity])
+            ytab[way, parity, 0] = high
+            ytab[way, parity, 1] = low
+            high, low = halves(wide_z[way, parity])
+            ztab[way, parity, :nz] = high
+            ztab[way, parity, nz:] = low
     for offset in range(1, n_kz):
         other = lax.rem(kz + offset, n_kz)
         for copy in point_copies(other, other):
@@ -289,13 +321,6 @@
             )
             scatter_lanes([got_a[s, four:] for s in sources], 1, rows, width, store_to([(s_maps, 2)], k, h))
 
-    for offset in range(1, COIL_GROUPS):
-        other = lax.rem(group + offset, COIL_GROUPS)
-        for copy in bin_copies(other, other):
-            copy.wait_send()
-            copy.wait_recv()
-        pair_copy(other, core).start()
-
     g_maps[...] = jnp.zeros_like(g_maps)
     g_coils[...] = jnp.zeros_like(g_coils)
 
@@ -303,15 +328,17 @@
         def body(offset, carry):
             other = lax.rem(group + offset, COIL_GROUPS)
             if c == 0:
-                @pl.when(offset > 0)
-                def _():
+                if not isinstance(offset, int):
                     pair_copy(other, core).wait_send()
                     pair_copy(other, 1 - core).wait_recv()
+                bits = jnp.concatenate([got_mask[other, 0], got_mask[other, 1]], axis=0)
+                bits = dot(bits.astype(jnp.float32).astype(jnp.bfloat16), order_y[...])
+                bits = jnp.concatenate([bits[:nz], bits[nz:]], axis=1).astype(jnp.bfloat16)
+                kept_masks[other] = dot(order_z[...], bits)
 
             amplitude = p_maps[1]
             model = []
             rows_in = []
-            kept = []
             for b in range(2):
                 tau = got_times[other, b, 0:1, 0:1]
                 decays = jnp.exp(-tau * p_maps[2])
@@ -322,28 +349,52 @@
                 imag = p_coils[2 * c + 1] * signal_step + s_coils[2 * c + 1] * signal
                 rows_in.append(jnp.concatenate([real, imag], axis=1))
                 model.append((decays, signal, slope))
-                kept.append(got_mask[other, b].astype(jnp.float32))
-            both = from_right(jnp.concatenate(rows_in, axis=0), ytab[0])
-            along_z = jnp.concatenate(
-                [
-                    jnp.concatenate([both[b * nz : (b + 1) * nz, :ny], both[b * nz : (b + 1) * nz, ny:]], axis=0)
-                    for b in range(2)
-                ],
-                axis=1,
-            )
-            kept = jnp.concatenate([jnp.concatenate(kept, axis=1)] * 2, axis=0)
-            back = from_left(ztab[1], from_left(ztab[0], along_z) * kept)
-            both = jnp.concatenate(
-                [
-                    jnp.concatenate([back[:nz, b * ny : (b + 1) * ny], back[nz:, b * ny : (b + 1) * ny]], axis=1)
-                    for b in range(2)
-                ],
-                axis=0,
-            )
-            back = from_right(both, ytab[1])
+            x = jnp.concatenate(rows_in, axis=0)
+            h = ny // 2
+            left, right = [jnp.concatenate([x[:, o : o + h], x[:, ny + o : ny + o + h]], axis=1) for o in (0, h)]
+            even = from_right(left + right, ytab[0, 0])
+            odd = from_right(left - right, ytab[0, 1])
+            parts_z = []
+            for o in (0, h):
+                parts_z.append(
+                    jnp.concatenate(
+                        [
+                            v
+                            for b in range(2)
+                            for v in (even[b * nz : (b + 1) * nz, o : o + h], odd[b * nz : (b + 1) * nz, o : o + h])
+                        ],
+                        axis=1,
+                    )
+                )
+            q = nz // 2
+            top = jnp.concatenate([v[:q] for v in parts_z], axis=0)
+            bottom = jnp.concatenate([v[q:] for v in parts_z], axis=0)
+            kept_even = kept_masks[other, :q]
+            kept_odd = kept_masks[other, q:]
+            even = from_left(ztab[0, 0], top + bottom) * jnp.concatenate([kept_even] * 2, axis=0)
+            odd = from_left(ztab[0, 1], top - bottom) * jnp.concatenate([kept_odd] * 2, axis=0)
+            even = from_left(ztab[1, 0], even)
+            odd = from_left(ztab[1, 1], odd)
+            top, bottom = even + odd, even - odd
+            real = jnp.concatenate([top[:q], bottom[:q]], axis=0)
+            imag = jnp.concatenate([top[q:], bottom[q:]], axis=0)
+            even, odd = [
+                jnp.concatenate(
+                    [
+                        jnp.concatenate([v[:, b * ny + o : b * ny + o + h] for v in (real, imag)], axis=1)
+                        for b in range(2)
+                    ],
+                    axis=0,
+                )
+                for o in (0, h)
+            ]
+            even = from_right(even, ytab[1, 0])
+            odd = from_right(odd, ytab[1, 1])
+            left, right = even + odd, even - odd
             for b, (decays, signal, slope) in enumerate(model):
-                real = back[b * nz : (b + 1) * nz, :ny]
-                imag = back[b * nz : (b + 1) * nz, ny:]
+                span = slice(b * nz, (b + 1) * nz)
+                real = jnp.concatenate([left[span, :h], right[span, :h]], axis=1)
+                imag = jnp.concatenate([left[span, h:], right[span, h:]], axis=1)
                 projected = p_coils[2 * c] * real + p_coils[2 * c + 1] * imag
                 g_coils[2 * c] += signal * real
                 g_coils[2 * c + 1] += signal * imag
@@ -352,7 +403,17 @@
                 g_maps[2] += slope * projected
             return carry
 
-        lax.fori_loop(0, COIL_GROUPS, body, 0)
+        if c == 0:
+            body(0, 0)
+            for offset in range(1, COIL_GROUPS):
+                other = lax.rem(group + offset, COIL_GROUPS)
+                for copy in bin_copies(other, other):
+                    copy.wait_send()
+                    copy.wait_recv()
+                pair_copy(other, core).start()
+            lax.fori_loop(1, COIL_GROUPS, body, 0)
+        else:
+            lax.fori_loop(0, COIL_GROUPS, body, 0)
 
     coil_pass(0)
 
@@ -431,19 +492,11 @@
     got_sums[me] = tile
     wait_all(sum_copy)
     whole = jnp.sum(got_sums[...], axis=0)
-    old, bend, cross, square = (whole[i : i + 1, :rows] for i in range(4))
+    old, bend, cross, square = (whole[i : i + 1, :] for i in range(4))
     step = old / bend
     ratio = (old - 2.0 * step * cross + step * step * square) / old
-    for x in range(n_kz):
-        for m in range(3):
-            r = res_maps[m, x] - step * app_maps[m, x]
-            new_res_maps[m, x] = r
-            new_dir_maps[m, x] = r + ratio * dir_maps[m, x]
-        for c in range(COIL_GROUPS * per_group):
-            for ri in range(2):
-                r = res_coils[ri, c, x] - step * app_coils[ri, c, x]
-                new_res_coils[ri, c, x] = r
-                new_dir_coils[ri, c, x] = r + ratio * dir_coils[ri, c, x]
+    scales[0] = jnp.broadcast_to(step, scales.shape[1:])
+    scales[1] = jnp.broadcast_to(ratio, scales.shape[1:])
 
 
 def shards(
@@ -458,12 +511,10 @@
     width = ny // n_ti
     local_bins, nz, _ = sampling_mask.shape
     f32 = jnp.float32
-    any_ = pl.BlockSpec(memory_space=pl.ANY)
     vmem = pl.BlockSpec(memory_space=pltpu.VMEM)
     dma = pltpu.SemaphoreType.DMA
-    times = jnp.broadcast_to(inversion_times[:, None, None], (local_bins, 8, LANES))
-    y_tables = jnp.asarray(np.stack(tables_y(ny)))
-    z_tables = jnp.asarray(np.stack(tables_z(nz)))
+    hbm = pl.BlockSpec(memory_space=pltpu.HBM)
+    tables = [jnp.asarray(t) for t in (tables_y(ny), tables_z(nz))]
     flipped = [
         jnp.swapaxes(a, -1, -2) for a in (direction_maps, direction_coils, residual_maps, residual_coils)
     ]
@@ -472,20 +523,26 @@
 
     outs = pl.pallas_call(
         functools.partial(step_kernel, n_ti, n_kz, per_group, four, one, two),
-        out_shape=[jax.ShapeDtypeStruct(flipped[i].shape, f32) for i in (2, 3, 0, 1)],
-        in_specs=[vmem] * 4 + [any_] * 6,
-        out_specs=[vmem] * 4,
+        out_shape=[jax.ShapeDtypeStruct(shape, f32) for shape in (flipped[0].shape, flipped[1].shape, (2, 8, LANES))],
+        in_specs=[hbm] * 6 + [pl.BlockSpec(memory_space=pltpu.SMEM)] + [hbm] * 3,
+        out_specs=[vmem] * 3,
         scratch_shapes=[
+            *(pltpu.VMEM(a.shape, f32) for a in flipped),
+            pltpu.VMEM((local_bins, 8, LANES), f32),
+            pltpu.VMEM((ny, ny), jnp.bfloat16),
+            pltpu.VMEM((nz, nz), jnp.bfloat16),
+            pltpu.VMEM((COIL_GROUPS, nz, 2 * ny), f32),
+            *(pltpu.VMEM(t.shape, f32) for t in tables),
             pltpu.VMEM((n_kz, COIL_GROUPS, a_rows, LANES), f32),
             pltpu.VMEM((n_kz, COIL_GROUPS, two, LANES), f32),
             pltpu.VMEM((total, a_rows, LANES), f32),
             pltpu.VMEM((total, two, LANES), f32),
             pltpu.VMEM((n_kz, 3, rows, ny), f32),
             pltpu.VMEM((n_kz, 2, per_group, rows, ny), f32),
-            pltpu.VMEM((COIL_GROUPS,) + times.shape, f32),
+            pltpu.VMEM((COIL_GROUPS, local_bins, 8, LANES), f32),
             pltpu.VMEM((COIL_GROUPS,) + sampling_mask.shape, jnp.int32),
-            pltpu.VMEM(y_tables.shape, jnp.bfloat16),
-            pltpu.VMEM(z_tables.shape, jnp.bfloat16),
+            pltpu.VMEM((2, 2, 2, ny, ny), jnp.bfloat16),
+            pltpu.VMEM((2, 2, 2 * nz, nz), jnp.bfloat16),
             pltpu.VMEM((3, nz, ny), f32),
             pltpu.VMEM((2 * per_group, nz, ny), f32),
             pltpu.VMEM((3, nz, ny), f32),
@@ -496,21 +553,23 @@
             pltpu.VMEM((total, two, LANES), f32),
             pltpu.VMEM((total, a_rows, LANES), f32),
             pltpu.VMEM((total, two, LANES), f32),
-            pltpu.VMEM(flipped[0].shape, f32),
-            pltpu.VMEM(flipped[1].shape, f32),
             pltpu.VMEM((8, LANES), f32),
             pltpu.VMEM((total, 8, LANES), f32),
         ]
         + [dma((total,))] * 10
         + [dma((n_kz,))] * 4
         + [dma((COIL_GROUPS,))] * 6
-        + [dma((6,))],
+        + [dma((9,))],
         compiler_params=pltpu.CompilerParams(
             collective_id=0, has_side_effects=True, vmem_limit_bytes=VMEM_LIMIT
         ),
         name="step",
-    )(*flipped, point_maps, point_coils, times, sampling_mask, y_tables, z_tables)
-    return tuple(jnp.swapaxes(a, -1, -2) for a in outs)
+    )(*flipped, point_maps, point_coils, inversion_times, sampling_mask, *tables)
+    applied = [jnp.swapaxes(a, -1, -2) for a in outs[:2]]
+    step, ratio = outs[2][0, 0, 0], outs[2][1, 0, 0]
+    new_residual = [r - step * a for r, a in zip((residual_maps, residual_coils), applied)]
+    new_direction = [r + ratio * d for r, d in zip(new_residual, (direction_maps, direction_coils))]
+    return (*new_residual, *new_direction)
 
 
 def solution(mesh):

time: 103 us -> 93.5 us (0.908)
  local copies, waits for them, and re-layouts: 10.3 us -> 1.29 us
  Pallas kernels: 91.6 us -> 84.9 us
  other arithmetic: 0 us -> 6.33 us
    unnamed x16 -> x10, local copies, waits for them, and re-layouts: 9.58 us -> 0.02 us
    pallas_call x1, Pallas kernels: 91.6 us -> 84.9 us  [shards(): pl.pallas_call(functools.partial(step_kernel, n_ti, n_kz, per_group, four...]
    add x0 -> x2, other arithmetic: none -> 6.33 us  [shards(): r + ratio * d]
    slice x0 -> x1, local copies, waits for them, and re-layouts: none -> 1.27 us  [shards(): step, ratio = (outs[2][0, 0, 0], outs[2][1, 0, 0])]
where the time goes in v3:
time: 93.5 us; the launch traced here: 93.3 us
  Pallas kernels  84.9 us (91%)
  other arithmetic  6.33 us (7%)
  local copies, waits for them, and re-layouts  1.29 us (1%)
    pallas_call x1, Pallas kernels, shards(): pl.pallas_call(functools.partial(step_kernel, n_ti, n_kz, per_group, four...  84.9 us
    add x2, other arithmetic, shards(): r + ratio * d  6.33 us

profile of v3, /device:TPU:0, one launch (start us, length us, event | category | flops | bytes accessed | tf_op | source)
XLA Modules:
  0.0 93.3 jit_solution(10391881772588307134)
XLA Ops:
  0.6 0.0 copy-start
  0.6 0.0 copy-start.1
  0.7 84.9 %step.1 = (f32[3,4,32,40]{3,2,1,0:T(8,128)}, f32[2,8,4,32,40]{4,3,2,1,0:T(8,128)}, f32[2,8,128]{2,1,0:T(8,128)}) custom-call(f32[3,4,32,40]{3,2,1,0:T(8,128)} %bitcast.14, f32[2,8,4,32,40]{4,3,2,1,0:T(8,128)} %bitcast.12, f32[3,4,32,40]{3,2,1,0:T(8,128)} %bitcast.15, f32[2,8,4,32,40]{4,3,2,1,0:T(8,128)} %bitcast.13, f32[3,4,40,256]{3,2,1,0:T(8,128)} %maps.1, ...), custom_call_target="tpu_custom_call" | custom-call | tf_op jit(solution)/shard_map/step/pallas_call | solution.py:524
  85.6 1.3 %fusion = (f32[1,1,1]{2,1,0:T(1,128)}, f32[1,1,1]{2,1,0:T(1,128)}) fusion(f32[2,8,128]{2,1,0:T(8,128)} %get-tuple-element.7), kind=kLoop, calls=%fused_computation.4 | loop fusion | bytes 16 | tf_op jit(solution)/shard_map/slice | solution.py:569
  86.9 0.0 copy-done
  86.9 0.0 copy-done.1
  86.9 0.0 copy-start.2
  86.9 0.0 copy-start.3
  86.9 0.0 copy-start.4
  86.9 4.3 %multiply_add_fusion = (f32[2,8,4,40,32]{3,4,2,1,0:T(8,128)}, f32[2,8,4,40,32]{3,4,2,1,0:T(8,128)}) fusion(f32[2,8,4,40,32]{3,4,2,1,0:T(8,128)S(1)} %copy-done, f32[]{:T(128)} %bitcast.7, f32[2,8,4,40,32]{3,4,2,1,0:T(8,128)S(1)} %copy-done.1, f32[2,8,4,32,40]{4,3,2,1,0:T(8,128)} %get-tuple-element.9, f32[]{:T(128)} %bitcast.4), kind=kLoop, calls=%fused_computation.1 | loop fusion | flops 327680 | bytes 1638408 | tf_op jit(solution)/shard_map/add | solution.py:571
  91.2 0.0 copy-done.2
  91.2 0.0 copy-done.3
  91.2 0.0 copy-done.4
  91.2 2.0 %multiply_add_fusion.1 = (f32[3,4,40,32]{2,3,1,0:T(8,128)}, f32[3,4,40,32]{2,3,1,0:T(8,128)}) fusion(f32[3,4,40,32]{2,3,1,0:T(8,128)S(1)} %copy-done.2, f32[]{:T(128)} %bitcast.7, f32[3,4,40,32]{2,3,1,0:T(8,128)S(1)} %copy-done.3, f32[3,4,32,40]{3,2,1,0:T(8,128)S(1)} %copy-done.4, f32[]{:T(128)} %bitcast.4), kind=kLoop, calls=%fused_computation.3 | loop fusion | flops 61440 | bytes 307208 | tf_op jit(solution)/shard_map/add | solution.py:571
Async XLA Ops:
  0.6 86.2 %copy-start = (f32[2,8,4,40,32]{3,4,2,1,0:T(8,128)S(1)}, f32[2,8,4,40,32]{3,4,2,1,0:T(8,128)}, u32[]{:S(2)}) copy-start(f32[2,8,4,40,32]{3,4,2,1,0:T(8,128)} %param.13) | copy-start | bytes 983044
  0.6 86.2 %copy-start.1 = (f32[2,8,4,40,32]{3,4,2,1,0:T(8,128)S(1)}, f32[2,8,4,40,32]{3,4,2,1,0:T(8,128)}, u32[]{:S(2)}) copy-start(f32[2,8,4,40,32]{3,4,2,1,0:T(8,128)} %param.15) | copy-start | bytes 983044
  86.9 4.4 %copy-start.2 = (f32[3,4,40,32]{2,3,1,0:T(8,128)S(1)}, f32[3,4,40,32]{2,3,1,0:T(8,128)}, u32[]{:S(2)}) copy-start(f32[3,4,40,32]{2,3,1,0:T(8,128)} %param.12) | copy-start | bytes 184324
  86.9 4.4 %copy-start.3 = (f32[3,4,40,32]{2,3,1,0:T(8,128)S(1)}, f32[3,4,40,32]{2,3,1,0:T(8,128)}, u32[]{:S(2)}) copy-start(f32[3,4,40,32]{2,3,1,0:T(8,128)} %param.14) | copy-start | bytes 184324
  86.9 4.3 %copy-start.4 = (f32[3,4,32,40]{3,2,1,0:T(8,128)S(1)}, f32[3,4,32,40]{3,2,1,0:T(8,128)}, u32[]{:S(2)}) copy-start(f32[3,4,32,40]{3,2,1,0:T(8,128)} %get-tuple-element.8) | copy-start | bytes 184324

commit v4 on v3

--- a/solution.py
+++ b/solution.py
@@ -138,7 +138,7 @@
 
 
 def step_kernel(
-    n_ti, n_kz, per_group, four, one, two,
+    n_ti, n_kz, per_group,
     dir_maps_in, dir_coils_in, res_maps_in, res_coils_in, maps, coils, bin_times, mask,
     tables_y_in, tables_z_in,
     app_maps, app_coils, scales,
@@ -146,7 +146,9 @@
     send_a, send_b, got_a, got_b, got_maps, got_coils, got_times, got_mask, ytab, ztab,
     p_maps, p_coils, s_maps, s_coils, g_maps, g_coils,
     back_a, back_b, ret_a, ret_b, sums, got_sums,
+    send_m, got_m, back_m, part_m, total_m, ret_m,
     a_out, a_in, b_out, b_in, ra_out, ra_in, rb_out, rb_in, sum_out, sum_in,
+    m_out, m_in, rm_out, rm_in, fm_out, fm_in, pm_out, pm_in,
     map_out, map_in, coil_out, coil_in, time_out, time_in, mask_out, mask_in, pair_out, pair_in, own,
 ):
     total = n_ti * n_kz
@@ -154,7 +156,10 @@
     kz = lax.axis_index("kz")
     me = ti * n_kz + kz
     group = lax.rem(ti, COIL_GROUPS)
-    first = (ti // COIL_GROUPS) * COIL_GROUPS
+    half = ti // COIL_GROUPS
+    n_half = n_ti // COIL_GROUPS
+    first = half * COIL_GROUPS
+    spot = half * n_kz + kz
     core = lax.rem(kz, 2)
     pair = kz + 1 - 2 * core
     width = dir_maps.shape[2]
@@ -200,14 +205,14 @@
         copy.wait()
 
     for x in range(n_kz):
-        last = fold([dir_maps[2, x]], width)
+        send_m[x] = fold([dir_maps[m, x] for m in range(3)], width)
         for g in range(COIL_GROUPS):
             c = g * per_group
-            send_a[x, g, :four] = fold([dir_coils[0, c, x], dir_coils[1, c, x], dir_maps[0, x], dir_maps[1, x]], width)
-            send_a[x, g, four:] = last
+            send_a[x, g] = fold([dir_coils[0, c, x], dir_coils[1, c, x]], width)
             send_b[x, g] = fold([dir_coils[0, c + 1, x], dir_coils[1, c + 1, x]], width)
     got_a[me] = send_a[kz, group]
     got_b[me] = send_b[kz, group]
+    got_m[group, spot] = send_m[kz]
 
     pl.semaphore_wait(barrier, total - 1)
 
@@ -268,10 +273,35 @@
         where = (ti, pair)
         return remote(got_mask.at[slot, plane], got_mask.at[slot, plane], pair_out.at[slot], pair_in.at[slot], where)
 
+    def m_copy(other, slot):
+        h, k = split_id(other)
+        where = (h * COIL_GROUPS + group, k)
+        return remote(send_m.at[k], got_m.at[group, slot], m_out.at[other], m_in.at[slot], where)
+
+    def rm_copy(other, slot):
+        h, k = split_id(other)
+        where = (h * COIL_GROUPS + group, k)
+        return remote(total_m.at[other], ret_m.at[slot], rm_out.at[other], rm_in.at[slot], where)
+
+    def fm_copy(other, slot):
+        return remote(got_m.at[slot], got_m.at[slot], fm_out.at[other], fm_in.at[slot], (first + other, kz))
+
+    def pm_copy(other, slot):
+        return remote(back_m.at[other], part_m.at[slot], pm_out.at[other], pm_in.at[slot], (first + other, kz))
+
+    spots = n_half * n_kz
+    for offset in range(1, spots):
+        m_copy(lax.rem(spot + offset, spots), spot).start()
     send_all(a_copy)
     for offset in range(1, n_kz):
         for copy in point_copies(lax.rem(kz + offset, n_kz), kz):
             copy.start()
+    for offset in range(1, spots):
+        other = lax.rem(spot + offset, spots)
+        m_copy(other, other).wait_send()
+        m_copy(other, other).wait_recv()
+    for offset in range(1, COIL_GROUPS):
+        fm_copy(lax.rem(group + offset, COIL_GROUPS), group).start()
     for offset in range(1, COIL_GROUPS):
         for copy in bin_copies(lax.rem(group + offset, COIL_GROUPS), group):
             copy.start()
@@ -302,6 +332,10 @@
             for ri in range(2):
                 p_coils[2 * c + ri, span, :] = got_coils[k, ri, c]
     wait_all(a_copy)
+    for offset in range(1, COIL_GROUPS):
+        other = lax.rem(group + offset, COIL_GROUPS)
+        fm_copy(other, group).wait_send()
+        fm_copy(other, other).wait_recv()
 
     def store_to(targets, k, h):
         def store(p, span, value):
@@ -315,11 +349,12 @@
     for k in range(n_kz):
         for h in range(tiles):
             sources = [(h * per_tile + j) * n_kz + k for j in range(per_tile)]
-            scatter_lanes(
-                [got_a[s, :four] for s in sources], 4, rows, width,
-                store_to(coil_zero + [(s_maps, 0), (s_maps, 1)], k, h),
-            )
-            scatter_lanes([got_a[s, four:] for s in sources], 1, rows, width, store_to([(s_maps, 2)], k, h))
+            scatter_lanes([got_a[s] for s in sources], 2, rows, width, store_to(coil_zero, k, h))
+            parts_m = []
+            for j in range(per_tile):
+                t = h * per_tile + j
+                parts_m.append(got_m[t % COIL_GROUPS, (t // COIL_GROUPS) * n_kz + k])
+            scatter_lanes(parts_m, 3, rows, width, store_to([(s_maps, m) for m in range(3)], k, h))
 
     g_maps[...] = jnp.zeros_like(g_maps)
     g_coils[...] = jnp.zeros_like(g_coils)
@@ -439,14 +474,29 @@
         span = slice(k * rows, (k + 1) * rows)
         for h in range(tiles):
             lanes = slice(h * LANES, (h + 1) * LANES)
-            planes = [g_coils[2, span, lanes], g_coils[3, span, lanes], g_maps[0, span, lanes], g_maps[1, span, lanes]]
-            final = [g_maps[2, span, lanes]]
+            planes = [g_maps[m, span, lanes] for m in range(3)]
             for j in range(per_tile):
-                to = (h * per_tile + j) * n_kz + k
-                back_a[to, :four] = collect_lanes(planes, j, rows, width)
-                back_a[to, four:] = collect_lanes(final, j, rows, width)
+                t = h * per_tile + j
+                back_m[t % COIL_GROUPS, (t // COIL_GROUPS) * n_kz + k] = collect_lanes(planes, j, rows, width)
+    for offset in range(1, COIL_GROUPS):
+        pm_copy(lax.rem(group + offset, COIL_GROUPS), group).start()
+    for k in range(n_kz):
+        span = slice(k * rows, (k + 1) * rows)
+        for h in range(tiles):
+            lanes = slice(h * LANES, (h + 1) * LANES)
+            planes = [g_coils[p, span, lanes] for p in (2, 3)]
+            for j in range(per_tile):
+                back_a[(h * per_tile + j) * n_kz + k] = collect_lanes(planes, j, rows, width)
     send_all(ra_copy)
     ret_a[me] = back_a[me]
+    others = [lax.rem(group + offset, COIL_GROUPS) for offset in range(1, COIL_GROUPS)]
+    for other in others:
+        pm_copy(other, group).wait_send()
+        pm_copy(other, other).wait_recv()
+    total_m[...] = (back_m[group] + part_m[others[0]]) + (part_m[others[1]] + part_m[others[2]])
+    for offset in range(1, spots):
+        rm_copy(lax.rem(spot + offset, spots), spot).start()
+    ret_m[spot] = total_m[spot]
     wait_all(rb_copy)
 
     parts = {"old": None, "bend": None, "cross": None, "square": None}
@@ -472,14 +522,16 @@
 
     wait_all(ra_copy)
     for x in range(n_kz):
-        summed = []
         for g in range(COIL_GROUPS):
-            block = added([ret_a[t * n_kz + x, :four] for t in range(g, n_ti, COIL_GROUPS)])
-            summed.append(block)
-            settle_coils(g * per_group + 1, x, unfold(block, 4, rows, width))
-        flat = unfold(added(summed), 4, rows, width)
-        final = unfold(added([ret_a[t * n_kz + x, four:] for t in range(n_ti)]), 1, rows, width)
-        grads = [flat[2 * width : 3 * width], flat[3 * width : 4 * width], final[:width]]
+            block = added([ret_a[t * n_kz + x] for t in range(g, n_ti, COIL_GROUPS)])
+            settle_coils(g * per_group + 1, x, unfold(block, 2, rows, width))
+    for offset in range(1, spots):
+        other = lax.rem(spot + offset, spots)
+        rm_copy(other, other).wait_send()
+        rm_copy(other, other).wait_recv()
+    for x in range(n_kz):
+        flat = unfold(added([ret_m[h * n_kz + x] for h in range(n_half)]), 3, rows, width)
+        grads = [flat[m * width : (m + 1) * width] for m in range(3)]
         for m, grad in enumerate(grads):
             app_maps[m, x] = settle(None, grad, dir_maps[m, x], res_maps[m, x])
 
@@ -497,6 +549,15 @@
     ratio = (old - 2.0 * step * cross + step * step * square) / old
     scales[0] = jnp.broadcast_to(step, scales.shape[1:])
     scales[1] = jnp.broadcast_to(ratio, scales.shape[1:])
+
+
+def finish_kernel(scales, app_maps, app_coils, dir_maps, dir_coils, res_maps, res_coils, *outs):
+    step = scales[0, 0:1, 0 : app_maps.shape[-1]]
+    ratio = scales[1, 0:1, 0 : app_maps.shape[-1]]
+    for i, (applied, d, r) in enumerate(((app_maps, dir_maps, res_maps), (app_coils, dir_coils, res_coils))):
+        updated = r[...] - step * applied[...]
+        outs[i][...] = updated
+        outs[2 + i][...] = updated + ratio * d[...]
 
 
 def shards(
@@ -518,11 +579,13 @@
     flipped = [
         jnp.swapaxes(a, -1, -2) for a in (direction_maps, direction_coils, residual_maps, residual_coils)
     ]
-    four, one, two = (lane_spans(rows, planes, width)[0] for planes in (4, 1, 2))
-    a_rows = four + one
+    two, three = (lane_spans(rows, planes, width)[0] for planes in (2, 3))
+    spots = (n_ti // COIL_GROUPS) * n_kz
+    x_maps = pltpu.VMEM((COIL_GROUPS, spots, three, LANES), f32)
+    y_maps = pltpu.VMEM((spots, three, LANES), f32)
 
     outs = pl.pallas_call(
-        functools.partial(step_kernel, n_ti, n_kz, per_group, four, one, two),
+        functools.partial(step_kernel, n_ti, n_kz, per_group),
         out_shape=[jax.ShapeDtypeStruct(shape, f32) for shape in (flipped[0].shape, flipped[1].shape, (2, 8, LANES))],
         in_specs=[hbm] * 6 + [pl.BlockSpec(memory_space=pltpu.SMEM)] + [hbm] * 3,
         out_specs=[vmem] * 3,
@@ -533,9 +596,9 @@
             pltpu.VMEM((nz, nz), jnp.bfloat16),
             pltpu.VMEM((COIL_GROUPS, nz, 2 * ny), f32),
             *(pltpu.VMEM(t.shape, f32) for t in tables),
-            pltpu.VMEM((n_kz, COIL_GROUPS, a_rows, LANES), f32),
             pltpu.VMEM((n_kz, COIL_GROUPS, two, LANES), f32),
-            pltpu.VMEM((total, a_rows, LANES), f32),
+            pltpu.VMEM((n_kz, COIL_GROUPS, two, LANES), f32),
+            pltpu.VMEM((total, two, LANES), f32),
             pltpu.VMEM((total, two, LANES), f32),
             pltpu.VMEM((n_kz, 3, rows, ny), f32),
             pltpu.VMEM((n_kz, 2, per_group, rows, ny), f32),
@@ -549,14 +612,18 @@
             pltpu.VMEM((2 * per_group, nz, ny), f32),
             pltpu.VMEM((3, nz, ny), f32),
             pltpu.VMEM((2 * per_group, nz, ny), f32),
-            pltpu.VMEM((total, a_rows, LANES), f32),
             pltpu.VMEM((total, two, LANES), f32),
-            pltpu.VMEM((total, a_rows, LANES), f32),
+            pltpu.VMEM((total, two, LANES), f32),
+            pltpu.VMEM((total, two, LANES), f32),
             pltpu.VMEM((total, two, LANES), f32),
             pltpu.VMEM((8, LANES), f32),
             pltpu.VMEM((total, 8, LANES), f32),
+            pltpu.VMEM((n_kz, three, LANES), f32),
+            x_maps, x_maps, x_maps, y_maps, y_maps,
         ]
         + [dma((total,))] * 10
+        + [dma((spots,))] * 4
+        + [dma((COIL_GROUPS,))] * 4
         + [dma((n_kz,))] * 4
         + [dma((COIL_GROUPS,))] * 6
         + [dma((9,))],
@@ -565,11 +632,18 @@
         ),
         name="step",
     )(*flipped, point_maps, point_coils, inversion_times, sampling_mask, *tables)
-    applied = [jnp.swapaxes(a, -1, -2) for a in outs[:2]]
-    step, ratio = outs[2][0, 0, 0], outs[2][1, 0, 0]
-    new_residual = [r - step * a for r, a in zip((residual_maps, residual_coils), applied)]
-    new_direction = [r + ratio * d for r, d in zip(new_residual, (direction_maps, direction_coils))]
-    return (*new_residual, *new_direction)
+    maps_block = pl.BlockSpec((3, 1, width, rows), lambda x: (0, x, 0, 0))
+    coils_block = pl.BlockSpec((2, coils, 1, width, rows), lambda x: (0, 0, x, 0, 0))
+    updated = pl.pallas_call(
+        finish_kernel,
+        out_shape=[jax.ShapeDtypeStruct(flipped[i].shape, f32) for i in (0, 1, 0, 1)],
+        grid=(n_kz,),
+        in_specs=[pl.BlockSpec((2, 8, LANES), lambda x: (0, 0, 0))] + [maps_block, coils_block] * 3,
+        out_specs=[maps_block, coils_block] * 2,
+        compiler_params=pltpu.CompilerParams(vmem_limit_bytes=VMEM_LIMIT),
+        name="finish",
+    )(outs[2], outs[0], outs[1], *flipped)
+    return tuple(jnp.swapaxes(a, -1, -2) for a in updated)
 
 
 def solution(mesh):

time: 93.5 us -> 87.4 us (0.935)
  other arithmetic: 6.33 us -> 0 us
  Pallas kernels: 84.9 us -> 86.6 us
  local copies, waits for them, and re-layouts: 1.29 us -> 0 us
    add x2 -> x0, other arithmetic: 6.33 us -> none  [shards(): r + ratio * d]
    pallas_call x1 -> x2, Pallas kernels: 84.9 us -> 86.6 us  [the longest x1 82.3 us: shards(): pl.pallas_call(functools.partial(step_kernel, n_ti, n_kz, per_group), out...]
    slice x1 -> x0, local copies, waits for them, and re-layouts: 1.27 us -> none  [shards(): step, ratio = (outs[2][0, 0, 0], outs[2][1, 0, 0])]
where the time goes in v4:
time: 87.4 us; the launch traced here: 87.2 us
  Pallas kernels  86.6 us (99%)
    pallas_call x1, Pallas kernels, shards(): pl.pallas_call(functools.partial(step_kernel, n_ti, n_kz, per_group), out...  82.3 us
    pallas_call x1, Pallas kernels, shards(): pl.pallas_call(finish_kernel, out_shape=[jax.ShapeDtypeStruct(flipped[i]....  4.21 us

profile of v4, /device:TPU:0, one launch (start us, length us, event | category | flops | bytes accessed | tf_op | source)
XLA Modules:
  0.0 87.2 jit_solution(2427124145526312865)
XLA Ops:
  0.6 82.3 %step.1 = (f32[3,4,32,40]{3,2,1,0:T(8,128)}, f32[2,8,4,32,40]{4,3,2,1,0:T(8,128)}, f32[2,8,128]{2,1,0:T(8,128)}) custom-call(f32[3,4,32,40]{3,2,1,0:T(8,128)} %bitcast.12, f32[2,8,4,32,40]{4,3,2,1,0:T(8,128)} %bitcast.8, f32[3,4,32,40]{3,2,1,0:T(8,128)} %bitcast.14, f32[2,8,4,32,40]{4,3,2,1,0:T(8,128)} %bitcast.10, f32[3,4,40,256]{3,2,1,0:T(8,128)} %maps.1, ...), custom_call_target="tpu_custom_call" | custom-call | tf_op jit(solution)/shard_map/step/pallas_call | solution.py:587
  83.0 4.2 %finish.1 = (f32[3,4,32,40]{3,2,1,0:T(8,128)}, f32[2,8,4,32,40]{4,3,2,1,0:T(8,128)}, f32[3,4,32,40]{3,2,1,0:T(8,128)}, f32[2,8,4,32,40]{4,3,2,1,0:T(8,128)}) custom-call(f32[2,8,128]{2,1,0:T(8,128)} %get-tuple-element.11.scales, f32[3,4,32,40]{3,2,1,0:T(8,128)} %get-tuple-element.12.app_maps, f32[2,8,4,32,40]{4,3,2,1,0:T(8,128)} %get-tuple-element.13.app_coils, ...), custom_call_target="tpu_custom_call" | custom-call | tf_op jit(solution)/shard_map/finish/pallas_call | solution.py:637

commit v5 on v4

--- a/solution.py
+++ b/solution.py
@@ -13,7 +13,7 @@
 regular_weight = 2.0
 COIL_GROUPS = 4
 LANES = 128
-VMEM_LIMIT = 60 * 1024 * 1024
+VMEM_LIMIT = 59 * 1024 * 1024
 
 
 def half_parts(length, parity):
@@ -209,9 +209,7 @@
         for g in range(COIL_GROUPS):
             c = g * per_group
             send_a[x, g] = fold([dir_coils[0, c, x], dir_coils[1, c, x]], width)
-            send_b[x, g] = fold([dir_coils[0, c + 1, x], dir_coils[1, c + 1, x]], width)
     got_a[me] = send_a[kz, group]
-    got_b[me] = send_b[kz, group]
     got_m[group, spot] = send_m[kz]
 
     pl.semaphore_wait(barrier, total - 1)
@@ -224,20 +222,20 @@
 
     def a_copy(other, slot):
         t, k = split_id(other)
-        return remote(send_a.at[k, lax.rem(t, COIL_GROUPS)], got_a.at[slot], a_out.at[other], a_in.at[slot], (t, k))
+        return remote(send_a.at[k, lax.rem(t, COIL_GROUPS)], got_a.at[slot], a_out, a_in, (t, k))
 
     def b_copy(other, slot):
         t, k = split_id(other)
-        return remote(send_b.at[k, lax.rem(t, COIL_GROUPS)], got_b.at[slot], b_out.at[other], b_in.at[slot], (t, k))
+        return remote(send_b.at[k, lax.rem(t, COIL_GROUPS)], got_b.at[slot], b_out, b_in, (t, k))
 
     def ra_copy(other, slot):
-        return remote(back_a.at[other], ret_a.at[slot], ra_out.at[other], ra_in.at[slot], split_id(other))
+        return remote(back_a.at[other], ret_a.at[slot], ra_out, ra_in, split_id(other))
 
     def rb_copy(other, slot):
-        return remote(back_b.at[other], ret_b.at[slot], rb_out.at[other], rb_in.at[slot], split_id(other))
+        return remote(back_b.at[other], ret_b.at[slot], rb_out, rb_in, split_id(other))
 
     def sum_copy(other, slot):
-        return remote(sums, got_sums.at[slot], sum_out.at[other], sum_in.at[slot], split_id(other))
+        return remote(sums, got_sums.at[slot], sum_out, sum_in, split_id(other))
 
     def send_all(copy):
         def body(offset, carry):
@@ -246,15 +244,9 @@
 
         lax.fori_loop(1, total, body, 0)
 
-    def wait_all(copy):
-        def body(offset, carry):
-            other = lax.rem(me + offset, total)
-            one_copy = copy(other, other)
-            one_copy.wait_send()
-            one_copy.wait_recv()
-            return carry
-
-        lax.fori_loop(1, total, body, 0)
+    def wait_bytes(slots, sem):
+        part = slots.at[pl.ds(0, total - 1)]
+        pltpu.make_async_copy(part, part, sem).wait()
 
     def point_copies(other, slot):
         return [
@@ -296,6 +288,11 @@
     for offset in range(1, n_kz):
         for copy in point_copies(lax.rem(kz + offset, n_kz), kz):
             copy.start()
+    for x in range(n_kz):
+        for g in range(COIL_GROUPS):
+            c = g * per_group + 1
+            send_b[x, g] = fold([dir_coils[0, c, x], dir_coils[1, c, x]], width)
+    got_b[me] = send_b[kz, group]
     for offset in range(1, spots):
         other = lax.rem(spot + offset, spots)
         m_copy(other, other).wait_send()
@@ -331,7 +328,7 @@
         for c in range(per_group):
             for ri in range(2):
                 p_coils[2 * c + ri, span, :] = got_coils[k, ri, c]
-    wait_all(a_copy)
+    wait_bytes(got_a, a_in)
     for offset in range(1, COIL_GROUPS):
         other = lax.rem(group + offset, COIL_GROUPS)
         fm_copy(other, group).wait_send()
@@ -462,7 +459,7 @@
     send_all(rb_copy)
     ret_b[me] = back_b[me]
 
-    wait_all(b_copy)
+    wait_bytes(got_b, b_in)
     for k in range(n_kz):
         for h in range(tiles):
             sources = [(h * per_tile + j) * n_kz + k for j in range(per_tile)]
@@ -497,7 +494,7 @@
     for offset in range(1, spots):
         rm_copy(lax.rem(spot + offset, spots), spot).start()
     ret_m[spot] = total_m[spot]
-    wait_all(rb_copy)
+    wait_bytes(ret_b, rb_in)
 
     parts = {"old": None, "bend": None, "cross": None, "square": None}
 
@@ -520,7 +517,7 @@
             block = added([ret_b[t * n_kz + x] for t in range(g, n_ti, COIL_GROUPS)])
             settle_coils(g * per_group, x, unfold(block, 2, rows, width))
 
-    wait_all(ra_copy)
+    wait_bytes(ret_a, ra_in)
     for x in range(n_kz):
         for g in range(COIL_GROUPS):
             block = added([ret_a[t * n_kz + x] for t in range(g, n_ti, COIL_GROUPS)])
@@ -542,7 +539,12 @@
     sums[...] = tile
     send_all(sum_copy)
     got_sums[me] = tile
-    wait_all(sum_copy)
+    wait_bytes(got_a, a_out)
+    wait_bytes(got_b, b_out)
+    wait_bytes(ret_a, ra_out)
+    wait_bytes(ret_b, rb_out)
+    wait_bytes(got_sums, sum_in)
+    wait_bytes(got_sums, sum_out)
     whole = jnp.sum(got_sums[...], axis=0)
     old, bend, cross, square = (whole[i : i + 1, :] for i in range(4))
     step = old / bend
@@ -621,7 +623,7 @@
             pltpu.VMEM((n_kz, three, LANES), f32),
             x_maps, x_maps, x_maps, y_maps, y_maps,
         ]
-        + [dma((total,))] * 10
+        + [dma] * 10
         + [dma((spots,))] * 4
         + [dma((COIL_GROUPS,))] * 4
         + [dma((n_kz,))] * 4
@@ -632,15 +634,12 @@
         ),
         name="step",
     )(*flipped, point_maps, point_coils, inversion_times, sampling_mask, *tables)
-    maps_block = pl.BlockSpec((3, 1, width, rows), lambda x: (0, x, 0, 0))
-    coils_block = pl.BlockSpec((2, coils, 1, width, rows), lambda x: (0, 0, x, 0, 0))
     updated = pl.pallas_call(
         finish_kernel,
         out_shape=[jax.ShapeDtypeStruct(flipped[i].shape, f32) for i in (0, 1, 0, 1)],
-        grid=(n_kz,),
-        in_specs=[pl.BlockSpec((2, 8, LANES), lambda x: (0, 0, 0))] + [maps_block, coils_block] * 3,
-        out_specs=[maps_block, coils_block] * 2,
-        compiler_params=pltpu.CompilerParams(vmem_limit_bytes=VMEM_LIMIT),
+        in_specs=[vmem] * 7,
+        out_specs=[vmem] * 4,
+        compiler_params=pltpu.CompilerParams(vmem_limit_bytes=16 * 1024 * 1024),
         name="finish",
     )(outs[2], outs[0], outs[1], *flipped)
     return tuple(jnp.swapaxes(a, -1, -2) for a in updated)

time: 87.4 us -> 84.8 us (0.970)
  Pallas kernels: 86.6 us -> 81 us
  local copies, waits for them, and re-layouts: 0 us -> 2.86 us
    pallas_call x1, Pallas kernels: 82.3 us -> 79.3 us  [shards(): pl.pallas_call(functools.partial(step_kernel, n_ti, n_kz, per_group), out...]
    unnamed x0 -> x14, local copies, waits for them, and re-layouts: none -> 2.86 us
    pallas_call x1, Pallas kernels: 4.21 us -> 1.67 us  [shards(): pl.pallas_call(finish_kernel, out_shape=[jax.ShapeDtypeStruct(flipped[i]....]
where the time goes in v5:
time: 84.8 us; the launch traced here: 84.5 us
  Pallas kernels  81 us (96%)
  local copies, waits for them, and re-layouts  2.86 us (3%)
    pallas_call x1, Pallas kernels, shards(): pl.pallas_call(functools.partial(step_kernel, n_ti, n_kz, per_group), out...  79.3 us
    unnamed x14, local copies, waits for them, and re-layouts  2.86 us

profile of v5, /device:TPU:0, one launch (start us, length us, event | category | flops | bytes accessed | tf_op | source)
XLA Modules:
  0.0 84.5 jit_solution(6512873562646595222)
XLA Ops:
  0.6 0.0 copy-start
  0.6 0.0 copy-start.1
  0.7 0.0 copy-start.3
  0.7 0.0 copy-start.4
  0.7 79.3 %step.1 = (f32[3,4,32,40]{3,2,1,0:T(8,128)}, f32[2,8,4,32,40]{4,3,2,1,0:T(8,128)}, f32[2,8,128]{2,1,0:T(8,128)}) custom-call(f32[3,4,32,40]{3,2,1,0:T(8,128)} %bitcast.12, f32[2,8,4,32,40]{4,3,2,1,0:T(8,128)} %bitcast.8, f32[3,4,32,40]{3,2,1,0:T(8,128)} %bitcast.14, f32[2,8,4,32,40]{4,3,2,1,0:T(8,128)} %bitcast.10, f32[3,4,40,256]{3,2,1,0:T(8,128)} %maps.1, ...), custom_call_target="tpu_custom_call" | custom-call | tf_op jit(solution)/shard_map/step/pallas_call | solution.py:589
  80.0 0.0 copy-done
  80.0 0.0 copy-done.1
  80.0 0.0 copy-done.3
  80.0 0.0 copy-done.4
  80.0 0.0 copy-start.2
  80.0 1.2 %copy-done.2 = f32[2,8,4,32,40]{4,3,2,1,0:T(8,128)S(1)} copy-done((f32[2,8,4,32,40]{4,3,2,1,0:T(8,128)S(1)}, f32[2,8,4,32,40]{4,3,2,1,0:T(8,128)}, u32[]{:S(2)}) %copy-start.2) | copy-done | bytes 327704
  81.2 0.0 copy-start.5
  81.2 0.9 %copy-done.5 = f32[3,4,32,40]{3,2,1,0:T(8,128)S(1)} copy-done((f32[3,4,32,40]{3,2,1,0:T(8,128)S(1)}, f32[3,4,32,40]{3,2,1,0:T(8,128)}, u32[]{:S(2)}) %copy-start.5) | copy-done | bytes 61464
  82.2 0.0 copy-start.6
  82.2 0.7 copy-done.6
  82.9 1.7 %finish.1 = (f32[3,4,32,40]{3,2,1,0:T(8,128)}, f32[2,8,4,32,40]{4,3,2,1,0:T(8,128)}, f32[3,4,32,40]{3,2,1,0:T(8,128)}, f32[2,8,4,32,40]{4,3,2,1,0:T(8,128)}) custom-call(f32[2,8,128]{2,1,0:T(8,128)S(1)} %copy-done.6, f32[3,4,32,40]{3,2,1,0:T(8,128)S(1)} %copy-done.5, f32[2,8,4,32,40]{4,3,2,1,0:T(8,128)S(1)} %copy-done.2, f32[3,4,32,40]{3,2,1,0:T(8,128)S(1)} %bitcast.13, ...), custom_call_target="tpu_custom_call" | custom-call | tf_op jit(solution)/shard_map/finish/pallas_call | solution.py:637
Async XLA Ops:
  0.6 79.3 %copy-start = (f32[2,8,4,40,32]{3,4,2,1,0:T(8,128)S(1)}, f32[2,8,4,40,32]{3,4,2,1,0:T(8,128)}, u32[]{:S(2)}) copy-start(f32[2,8,4,40,32]{3,4,2,1,0:T(8,128)} %param.13) | copy-start | bytes 983044
  0.6 79.3 %copy-start.1 = (f32[2,8,4,40,32]{3,4,2,1,0:T(8,128)S(1)}, f32[2,8,4,40,32]{3,4,2,1,0:T(8,128)}, u32[]{:S(2)}) copy-start(f32[2,8,4,40,32]{3,4,2,1,0:T(8,128)} %param.15) | copy-start | bytes 983044
  0.7 79.3 %copy-start.3 = (f32[3,4,40,32]{2,3,1,0:T(8,128)S(1)}, f32[3,4,40,32]{2,3,1,0:T(8,128)}, u32[]{:S(2)}) copy-start(f32[3,4,40,32]{2,3,1,0:T(8,128)} %param.12) | copy-start | bytes 184324
  0.7 79.3 %copy-start.4 = (f32[3,4,40,32]{2,3,1,0:T(8,128)S(1)}, f32[3,4,40,32]{2,3,1,0:T(8,128)}, u32[]{:S(2)}) copy-start(f32[3,4,40,32]{2,3,1,0:T(8,128)} %param.14) | copy-start | bytes 184324
  80.0 1.2 %copy-start.2 = (f32[2,8,4,32,40]{4,3,2,1,0:T(8,128)S(1)}, f32[2,8,4,32,40]{4,3,2,1,0:T(8,128)}, u32[]{:S(2)}) copy-start(f32[2,8,4,32,40]{4,3,2,1,0:T(8,128)} %get-tuple-element.13.app_coils) | copy-start | bytes 983044
  81.2 0.9 %copy-start.5 = (f32[3,4,32,40]{3,2,1,0:T(8,128)S(1)}, f32[3,4,32,40]{3,2,1,0:T(8,128)}, u32[]{:S(2)}) copy-start(f32[3,4,32,40]{3,2,1,0:T(8,128)} %get-tuple-element.12.app_maps) | copy-start | bytes 184324
  82.2 0.7 copy-start.6

commit v6 on v5

--- a/solution.py
+++ b/solution.py
@@ -634,12 +634,16 @@
         ),
         name="step",
     )(*flipped, point_maps, point_coils, inversion_times, sampling_mask, *tables)
+    def whole(array):
+        return pl.BlockSpec(array.shape, lambda i: (0,) * array.ndim)
+
     updated = pl.pallas_call(
         finish_kernel,
         out_shape=[jax.ShapeDtypeStruct(flipped[i].shape, f32) for i in (0, 1, 0, 1)],
-        in_specs=[vmem] * 7,
-        out_specs=[vmem] * 4,
-        compiler_params=pltpu.CompilerParams(vmem_limit_bytes=16 * 1024 * 1024),
+        grid=(1,),
+        in_specs=[whole(outs[2]), whole(outs[0]), whole(outs[1])] + [vmem] * 4,
+        out_specs=[whole(flipped[i]) for i in (0, 1, 0, 1)],
+        compiler_params=pltpu.CompilerParams(vmem_limit_bytes=61 * 1024 * 1024),
         name="finish",
     )(outs[2], outs[0], outs[1], *flipped)
     return tuple(jnp.swapaxes(a, -1, -2) for a in updated)

time: 84.8 us -> 83.7 us (0.987)
  local copies, waits for them, and re-layouts: 2.86 us -> 0 us
  Pallas kernels: 81 us -> 82.9 us
    unnamed x14 -> x0, local copies, waits for them, and re-layouts: 2.86 us -> none
    pallas_call x1, Pallas kernels: 1.67 us -> 3.76 us  [shards(): pl.pallas_call(finish_kernel, out_shape=[jax.ShapeDtypeStruct(flipped[i]....]
where the time goes in v6:
time: 83.7 us; the launch traced here: 83.6 us
  Pallas kernels  82.9 us (99%)
    pallas_call x1, Pallas kernels, shards(): pl.pallas_call(functools.partial(step_kernel, n_ti, n_kz, per_group), out...  79.2 us
    pallas_call x1, Pallas kernels, shards(): pl.pallas_call(finish_kernel, out_shape=[jax.ShapeDtypeStruct(flipped[i]....  3.76 us

profile of v6, /device:TPU:0, one launch (start us, length us, event | category | flops | bytes accessed | tf_op | source)
XLA Modules:
  0.0 83.6 jit_solution(556112272856335965)
XLA Ops:
  0.6 79.2 %step.1 = (f32[3,4,32,40]{3,2,1,0:T(8,128)}, f32[2,8,4,32,40]{4,3,2,1,0:T(8,128)}, f32[2,8,128]{2,1,0:T(8,128)}) custom-call(f32[3,4,32,40]{3,2,1,0:T(8,128)} %bitcast.12, f32[2,8,4,32,40]{4,3,2,1,0:T(8,128)} %bitcast.8, f32[3,4,32,40]{3,2,1,0:T(8,128)} %bitcast.14, f32[2,8,4,32,40]{4,3,2,1,0:T(8,128)} %bitcast.10, f32[3,4,40,256]{3,2,1,0:T(8,128)} %maps.1, ...), custom_call_target="tpu_custom_call" | custom-call | tf_op jit(solution)/shard_map/step/pallas_call | solution.py:589
  79.8 3.8 %finish.1 = (f32[3,4,32,40]{3,2,1,0:T(8,128)}, f32[2,8,4,32,40]{4,3,2,1,0:T(8,128)}, f32[3,4,32,40]{3,2,1,0:T(8,128)}, f32[2,8,4,32,40]{4,3,2,1,0:T(8,128)}) custom-call(f32[2,8,128]{2,1,0:T(8,128)} %get-tuple-element.11.scales, f32[3,4,32,40]{3,2,1,0:T(8,128)} %get-tuple-element.12.app_maps, f32[2,8,4,32,40]{4,3,2,1,0:T(8,128)} %get-tuple-element.13.app_coils, ...), custom_call_target="tpu_custom_call" | custom-call | tf_op jit(solution)/shard_map/finish/pallas_call | solution.py:640
